TPU v7x, 32 devices: a whole 2x2x4 slice. The times are simulated.
32 devices in a mesh: groups: 2 (over y), seq: 4 (over z), head: 4 (over x, core).
Axes of the slice: x: 2, y: 2, z: 4, core: 2. Of those that a mesh axis runs over, the one named last changes fastest.
Arguments:
- tokens: bfloat16 [2048, 4096], P(('groups', 'seq'), 'head'), parts along dimension 0, may hold values from -6 to 6
- norm_gain: float32 [4096], replicated, may hold values from 0.1 to 1.9
- w_query: bfloat16 [4096, 4096], P('seq', 'head'), may hold values from -0.09375 to 0.09375
- w_key: bfloat16 [4096, 4096], P('seq', 'head'), may hold values from -0.1875 to 0.1875
- w_value: bfloat16 [4096, 4096], P('seq', 'head'), may hold values from -0.09375 to 0.09375
- w_out: bfloat16 [4096, 4096], P('seq', 'head'), may hold values from -0.375 to 0.375
- database: bfloat16 [64, 128, 4096], P(('groups', 'seq'), None, 'head'), parts along dimension 0, may hold values from -6 to 6
- nbr_shard: int32 [32, 2], P(('groups', 'seq')), parts along dimension 0, may hold values from 0 to 3, all different within a row; in each aligned block of 4 rows (0 to 3, 4 to 7, ...) at most 4 rows name the same one
- nbr_row: int32 [32, 2], P(('groups', 'seq')), parts along dimension 0, may hold values from 0 to 7
Outputs:
- attended: bfloat16 [2048, 4096], P(('groups', 'seq'), 'head'), parts along dimension 0
There are 2 independent parts, one for each index of `groups`. A program takes and returns all parts, laid end to end along the dimension named above; an argument that names none is the same for every part. Nothing has to cross between parts.
Inputs may be any that keep to these rules, and one draw needn't show every extreme that they name: `nbr_shard`: each span's two neighbours come from two different shards. Among the 4 spans of one index of seq, no shard is named more than 4 times, a bound that some block reaches.
All inputs are finite; a program needn't handle non-finite values.
Results may differ from a plain program's by a relative error of at most 0.012.
Values may be sent and summed in bfloat16 or wider, within the bound.
A program may use at most 128 MiB of HBM per device.

v0:
```python
import jax
import jax.numpy as jnp
from jax import lax
from jax.sharding import PartitionSpec as P

HD = 128


def local(tokens, norm_gain, w_query, w_key, w_value, w_out, database, nbr_shard, nbr_row):
    whole = lax.all_gather(tokens, "head", axis=1, tiled=True)
    x = whole.astype(jnp.float32)
    inverse = lax.rsqrt(jnp.mean(x * x, axis=-1, keepdims=True) + 1e-06)
    normed = (x * inverse * norm_gain).astype(jnp.bfloat16)
    tok_rows = normed.shape[0]
    width = w_query.shape[1]
    heads_dev = width // HD
    query = jnp.dot(
        normed,
        lax.all_gather(w_query, "seq", axis=0, tiled=True),
        preferred_element_type=jnp.float32,
    )
    query = (query / jnp.sqrt(jnp.float32(HD))).astype(jnp.bfloat16)
    num_seq = lax.axis_size("seq")
    spans_dev = nbr_shard.shape[0]
    count = 2 * spans_dev
    capacity = max(2, 4 * spans_dev // num_seq)
    shard_flat = nbr_shard.reshape(-1)
    row_flat = nbr_row.reshape(-1)
    positions = jnp.arange(count, dtype=jnp.int32)
    earlier = positions[None, :] < positions[:, None]
    slot_flat = jnp.sum(earlier & (shard_flat[:, None] == shard_flat[None, :]), axis=1)
    owners = jnp.arange(num_seq, dtype=jnp.int32)
    slots = jnp.arange(capacity, dtype=jnp.int32)
    match = (shard_flat[:, None, None] == owners[None, :, None]) & (
        slot_flat[:, None, None] == slots[None, None, :]
    )
    wanted = jnp.sum(jnp.where(match, row_flat[:, None, None], 0), axis=0)
    asked = lax.all_to_all(wanted, "seq", split_axis=0, concat_axis=0, tiled=True)
    ntok = database.shape[1]
    feat_dev = database.shape[2]
    wanted_slots = shard_flat * capacity + slot_flat
    outgoing = jnp.take(database, asked.reshape(-1), axis=0)
    outgoing = outgoing.reshape(num_seq, capacity, ntok, feat_dev)
    arrived = lax.all_to_all(outgoing, "seq", split_axis=0, concat_axis=0, tiled=True)
    arrived = arrived.reshape(num_seq * capacity, ntok, feat_dev)
    picked = jnp.take(arrived, wanted_slots, axis=0)
    key_full, value_full = (
        lax.all_gather(w_key, "seq", axis=0, tiled=True),
        lax.all_gather(w_value, "seq", axis=0, tiled=True),
    )
    piece = lax.all_gather(picked, "head", axis=2, tiled=True)
    flat = piece.reshape(-1, piece.shape[2])
    keys = jnp.dot(flat, key_full, preferred_element_type=jnp.float32)
    values = jnp.dot(flat, value_full, preferred_element_type=jnp.float32)
    keys = keys.astype(jnp.bfloat16)
    values = values.astype(jnp.bfloat16)
    keys = keys.reshape(spans_dev, 2 * ntok, heads_dev, HD)
    values = values.reshape(spans_dev, 2 * ntok, heads_dev, HD)
    span_len = tok_rows // spans_dev
    qh = query.reshape(spans_dev, span_len, heads_dev, HD)
    scores = jnp.einsum("cqhd,ckhd->chqk", qh, keys, preferred_element_type=jnp.float32)
    weights = jax.nn.softmax(scores, axis=-1).astype(jnp.bfloat16)
    context = jnp.einsum("chqk,ckhd->cqhd", weights, values, preferred_element_type=jnp.float32)
    context = context.astype(jnp.bfloat16).reshape(tok_rows, width)
    out_full = lax.all_gather(w_out, "seq", axis=0, tiled=True)
    attended = jnp.dot(
        lax.all_gather(context, "head", axis=1, tiled=True),
        out_full,
        preferred_element_type=jnp.float32,
    )
    return attended.astype(jnp.bfloat16)


def solution(mesh):
    return jax.shard_map(
        local,
        mesh=mesh,
        in_specs=(
            P(("groups", "seq"), "head"),
            P(),
            P("seq", "head"),
            P("seq", "head"),
            P("seq", "head"),
            P("seq", "head"),
            P(("groups", "seq"), None, "head"),
            P(("groups", "seq"), None),
            P(("groups", "seq"), None),
        ),
        out_specs=P(("groups", "seq"), "head"),
        check_vma=False,
    )
```

profile of v0, /device:TPU:0, one launch (start us, length us, event | category | flops | bytes accessed | tf_op | source)
XLA Modules:
  0.0 807.2 jit_solution(15849428937810329458)
XLA Ops:
  6.5 0.7 all-gather.12.cloned.1.call-update
  7.3 0.7 all-gather.14.cloned.1.call-update
  8.1 0.7 all-gather.10.cloned.1.call-update
  9.5 11.7 %all_to_all.14 = s32[4,1,4]{2,1,0:T(1,128)S(1)} all-to-all(s32[4,1,4]{2,1,0:T(1,128)S(1)} %bitcast.50), channel_id=1, replica_groups=mesh['groups'=2,'seq'=4,'head'=4] {'seq'}, dimensions={0} | all-to-all | bytes 128 | tf_op jit(solution)/shard_map/all_to_all | solution.py:38
  21.2 0.5 broadcast.146
  21.7 0.7 reduce.3
  22.4 2.8 gather_fusion
  25.2 4.6 broadcast_select_fusion
  29.9 4.9 all-to-all-start.1
  35.0 198.6 %all-to-all-done.1 = bf16[4,4,128,1024]{3,2,1,0:T(8,128)(2,1)} async-done(((bf16[4,4,128,1024]{3,2,1,0:T(8,128)(2,1)}), bf16[4,4,128,1024]{3,2,1,0:T(8,128)(2,1)}, u32[]{:S(2)}, u32[]{:S(2)}) %all-to-all-start.1) | async-done | bytes 4194336 | tf_op jit(solution)/shard_map/all_to_all | solution.py:44
  233.6 2.9 gather_fusion.1
  236.5 1.6 broadcast_select_fusion.1
  238.2 0.5 all-gather.16.cloned.1.call-update
  238.8 0.5 all-gather.20.cloned.1.call-update
  239.4 2.2 fusion.1
  241.6 20.3 %all-gather.14.cloned.1.call-done = bf16[4096,1024]{1,0:T(8,128)(2,1)} async-done(((bf16[1024,1024]{1,0:T(8,128)(2,1)}), bf16[4096,1024]{1,0:T(8,128)(2,1)}) %all-gather.14.cloned.1.call-update) | async-done | bytes 8388624 | tf_op jit(solution)/shard_map/all_gather | solution.py:19
  261.9 5.8 fusion.21
  267.8 144.5 %all-gather.10.cloned.1.call-done = bf16[4096,1024]{1,0:T(8,128)(2,1)} async-done(((bf16[1024,1024]{1,0:T(8,128)(2,1)}), bf16[4096,1024]{1,0:T(8,128)(2,1)}) %all-gather.10.cloned.1.call-update) | async-done | bytes 8388624 | tf_op jit(solution)/shard_map/all_gather | solution.py:49
  412.3 58.0 %all-gather.8.cloned.1.call-done = bf16[8,128,4096]{2,1,0:T(8,128)(2,1)} async-done(((bf16[8,128,1024]{2,1,0:T(8,128)(2,1)}), bf16[8,128,4096]{2,1,0:T(8,128)(2,1)}) %all-gather.8.cloned.1.call-update) | async-done | bytes 8388624 | tf_op jit(solution)/shard_map/all_gather | solution.py:51
  470.3 13.7 %convert_bitcast_fusion.1 = bf16[128,8,8,128]{3,1,2,0:T(8,128)(2,1)S(1)} fusion(bf16[1024,4096]{1,0:T(8,128)(2,1)} %bitcast.51, bf16[4096,1024]{1,0:T(8,128)(2,1)} %all-gather.10.cloned.1.call-done), kind=kOutput, calls=%fused_computation.19 | convolution fusion | flops 8590983168 | bytes 18874368 | tf_op jit(solution)/shard_map/dot_general | solution.py:54
  483.9 2.0 copy.41
  485.9 135.4 %all-gather.16.cloned.1.call-done = bf16[4096,1024]{1,0:T(8,128)(2,1)} async-done(((bf16[1024,1024]{1,0:T(8,128)(2,1)}), bf16[4096,1024]{1,0:T(8,128)(2,1)}) %all-gather.16.cloned.1.call-update) | async-done | bytes 8388624 | tf_op jit(solution)/shard_map/all_gather | solution.py:48
  621.4 13.8 %convert_bitcast_fusion = bf16[128,8,8,128]{3,1,2,0:T(8,128)(2,1)S(1)} fusion(bf16[1024,4096]{1,0:T(8,128)(2,1)} %bitcast.52, bf16[4096,1024]{1,0:T(8,128)(2,1)} %all-gather.16.cloned.1.call-done), kind=kOutput, calls=%fused_computation.16 | convolution fusion | flops 8590983168 | bytes 18874368 | tf_op jit(solution)/shard_map/dot_general | solution.py:53
  635.2 0.6 copy.40
  635.8 0.9 fusion.8
  636.7 0.6 fusion.33
  637.3 5.2 fusion.24
  642.6 0.3 copy.38
  642.9 0.9 copy.54
  643.8 126.8 %all-gather.20.cloned.1.call-done = bf16[4096,1024]{1,0:T(8,128)(2,1)} async-done(((bf16[1024,1024]{1,0:T(8,128)(2,1)}), bf16[4096,1024]{1,0:T(8,128)(2,1)}) %all-gather.20.cloned.1.call-update) | async-done | bytes 8388624 | tf_op jit(solution)/shard_map/all_gather | solution.py:65
  770.7 22.4 %all-gather.18.cloned.1.call-done = bf16[256,4096]{1,0:T(8,128)(2,1)} async-done(((bf16[256,1024]{1,0:T(8,128)(2,1)}), bf16[256,4096]{1,0:T(8,128)(2,1)}) %all-gather.18.cloned.1.call-update) | async-done | bytes 2097168 | tf_op jit(solution)/shard_map/all_gather | solution.py:67
  793.1 7.3 convolution_convert_fusion
  (41 shorter events, 1.4 us)
Async XLA Ops:
  6.5 15.9 %copy-start = (bf16[8,128,1024]{2,1,0:T(8,128)(2,1)S(1)}, bf16[8,128,1024]{2,1,0:T(8,128)(2,1)}, u32[]{:S(2)}) copy-start(bf16[8,128,1024]{2,1,0:T(8,128)(2,1)} %param.15) | copy-start | bytes 6291460
  6.5 232.8 %all-gather.12.cloned.1.call-start = ((), (), s32[]{:S(2)}) async-start(), calls=%async_computation.4 | async-start | bytes 2621440 | tf_op jit(solution)/shard_map/all_gather | solution.py:10
  7.3 1.5 copy-start.4
  7.3 1.7 copy-start.3
  7.3 254.7 %all-gather.14.cloned.1.call-start = ((), (), s32[]{:S(2)}) async-start(), calls=%async_computation.5 | async-start | bytes 10485760 | tf_op jit(solution)/shard_map/all_gather | solution.py:19
  8.0 404.3 %all-gather.10.cloned.1.call-start = ((), (), s32[]{:S(2)}) async-start(), calls=%async_computation.3 | async-start | bytes 10485760 | tf_op jit(solution)/shard_map/all_gather | solution.py:49
  29.9 203.8 %all-to-all-start.1 = ((bf16[4,4,128,1024]{3,2,1,0:T(8,128)(2,1)}), bf16[4,4,128,1024]{3,2,1,0:T(8,128)(2,1)}, u32[]{:S(2)}, u32[]{:S(2)}) async-start(bf16[4,4,128,1024]{3,2,1,0:T(8,128)(2,1)} %broadcast_select_fusion), calls=%async_computation.1 | async-start | bytes 8388608 | tf_op jit(solution)/shard_map/all_to_all | solution.py:44
  34.7 435.6 %all-gather.8.cloned.1.call-start = ((), (), s32[]{:S(2)}) async-start(), calls=%async_computation.2 | async-start | bytes 10485760 | tf_op jit(solution)/shard_map/all_gather | solution.py:51
  238.1 383.2 %all-gather.16.cloned.1.call-start = ((), (), s32[]{:S(2)}) async-start(), calls=%async_computation.6 | async-start | bytes 10485760 | tf_op jit(solution)/shard_map/all_gather | solution.py:48
  238.7 23.2 %copy-start.5 = (f32[4096]{0:T(1024)S(1)}, f32[4096]{0:T(1024)}, u32[]{:S(2)}) copy-start(f32[4096]{0:T(1024)} %param.10) | copy-start | bytes 49156
  238.7 532.0 %all-gather.20.cloned.1.call-start = ((), (), s32[]{:S(2)}) async-start(), calls=%async_computation.8 | async-start | bytes 10485760 | tf_op jit(solution)/shard_map/all_gather | solution.py:65
  239.3 553.8 %all-gather.18.cloned.1.call-start = ((), (), s32[]{:S(2)}) async-start(), calls=%async_computation.7 | async-start | bytes 2621440 | tf_op jit(solution)/shard_map/all_gather | solution.py:67
  239.4 22.6 %copy-start.2 = (bf16[256,4096]{1,0:T(8,128)(2,1)S(1)}, bf16[256,4096]{1,0:T(8,128)(2,1)}, u32[]{:S(2)}) copy-start(bf16[256,4096]{1,0:T(8,128)(2,1)} %all-gather.12.cloned.1.call-done) | copy-start | bytes 6291460
  793.1 7.3 copy-start.1
Sparse Core Ops, SparseCore 0:
  8.9 25.2 all-gather.11
  35.8 226.0 all-gather.13
  263.5 148.7 all-gather.9
  413.7 56.4 all-gather.7
  471.7 149.6 all-gather.15
  622.8 147.8 all-gather.19
  772.2 20.7 all-gather.17
where the time goes:
time: 808 us; the launch traced here: 807 us
  waiting for transfers between devices  709 us (88%)
  matrix products  46.7 us (6%)
  between operations  13.6 us (2%)
  blocking collectives  11.7 us (1%)
  local copies, waits for them, and re-layouts  10.8 us (1%)
  other arithmetic  10.1 us (1%)
    all_to_all x1, waiting for transfers between devices, local(): lax.all_to_all(outgoing, 'seq', split_axis=0, concat_axis=0, tiled=True)  199 us
    all_gather x1, waiting for transfers between devices, local(): lax.all_gather(w_value, 'seq', axis=0, tiled=True)  144 us
    all_gather x1, waiting for transfers between devices, local(): lax.all_gather(w_key, 'seq', axis=0, tiled=True)  135 us
    all_gather x1, waiting for transfers between devices, local(): out_full = lax.all_gather(w_out, 'seq', axis=0, tiled=True)  127 us
    all_gather x1, waiting for transfers between devices, local(): piece = lax.all_gather(picked, 'head', axis=2, tiled=True)  58 us
    all_gather x1, waiting for transfers between devices, local(): lax.all_gather(context, 'head', axis=1, tiled=True)  22.4 us
    all_gather x1, waiting for transfers between devices, local(): lax.all_gather(w_query, 'seq', axis=0, tiled=True)  20.3 us
  transfers between devices with their start and end apart: 8, of which 7 were waited for; matrix products, arithmetic and copies ran while one was open for 7% of the time, Pallas kernels for 0%

commit v1 on v0

--- a/solution.py
+++ b/solution.py
@@ -4,6 +4,13 @@
 from jax.sharding import PartitionSpec as P
 
 HD = 128
+
+
+def gather_rows(weight):
+    parts = lax.axis_size("groups")
+    rows = weight.shape[0] // parts
+    half = lax.dynamic_slice_in_dim(weight, lax.axis_index("groups") * rows, rows, axis=0)
+    return lax.all_gather(half, ("seq", "groups"), axis=0, tiled=True)
 
 
 def local(tokens, norm_gain, w_query, w_key, w_value, w_out, database, nbr_shard, nbr_row):
@@ -16,7 +23,7 @@
     heads_dev = width // HD
     query = jnp.dot(
         normed,
-        lax.all_gather(w_query, "seq", axis=0, tiled=True),
+        gather_rows(w_query),
         preferred_element_type=jnp.float32,
     )
     query = (query / jnp.sqrt(jnp.float32(HD))).astype(jnp.bfloat16)
@@ -45,8 +52,8 @@
     arrived = arrived.reshape(num_seq * capacity, ntok, feat_dev)
     picked = jnp.take(arrived, wanted_slots, axis=0)
     key_full, value_full = (
-        lax.all_gather(w_key, "seq", axis=0, tiled=True),
-        lax.all_gather(w_value, "seq", axis=0, tiled=True),
+        gather_rows(w_key),
+        gather_rows(w_value),
     )
     piece = lax.all_gather(picked, "head", axis=2, tiled=True)
     flat = piece.reshape(-1, piece.shape[2])
@@ -62,7 +69,7 @@
     weights = jax.nn.softmax(scores, axis=-1).astype(jnp.bfloat16)
     context = jnp.einsum("chqk,ckhd->cqhd", weights, values, preferred_element_type=jnp.float32)
     context = context.astype(jnp.bfloat16).reshape(tok_rows, width)
-    out_full = lax.all_gather(w_out, "seq", axis=0, tiled=True)
+    out_full = gather_rows(w_out)
     attended = jnp.dot(
         lax.all_gather(context, "head", axis=1, tiled=True),
         out_full,

time: 808 us -> 705 us (0.87)
  waiting for transfers between devices: 709 us -> 597 us
  local copies, waits for them, and re-layouts: 10.8 us -> 20.2 us
    all_gather x4, waiting for transfers between devices: 427 us -> 356 us  [gather_rows(): return lax.all_gather(half, ('seq', 'groups'), axis=0, tiled=True)]
    all_to_all x1, waiting for transfers between devices: 199 us -> 160 us  [local(): lax.all_to_all(outgoing, 'seq', split_axis=0, concat_axis=0, tiled=True)]
  transfers between devices with their start and end apart: 8 -> 8, of which waited for: 7 -> 7; matrix products, arithmetic and copies ran while one was open for 7% -> 10% of each run, Pallas kernels for 0% -> 0%
where the time goes in v1:
time: 705 us
  waiting for transfers between devices  597 us (85%)
  matrix products  46.7 us (7%)
  local copies, waits for them, and re-layouts  20.2 us (3%)
  between operations  13.6 us (2%)
  blocking collectives  11.7 us (2%)
  other arithmetic  10.1 us (1%)
    all_gather x4, waiting for transfers between devices, gather_rows(): return lax.all_gather(half, ('seq', 'groups'), axis=0, tiled=True)  356 us
    all_to_all x1, waiting for transfers between devices, local(): lax.all_to_all(outgoing, 'seq', split_axis=0, concat_axis=0, tiled=True)  160 us
    all_gather x1, waiting for transfers between devices, local(): piece = lax.all_gather(picked, 'head', axis=2, tiled=True)  57.9 us
    all_gather x1, waiting for transfers between devices, local(): lax.all_gather(context, 'head', axis=1, tiled=True)  22.4 us
  transfers between devices with their start and end apart: 8, of which 7 were waited for; matrix products, arithmetic and copies ran while one was open for 10% of the time, Pallas kernels for 0%

profile of v1, /device:TPU:0, one launch (start us, length us, event | category | flops | bytes accessed | tf_op | source)
XLA Modules:
  0.0 704.6 jit_solution(11762270696132331283)
XLA Ops:
  6.5 0.7 all-gather.12.cloned.1.call-update
  7.3 2.3 constant_dynamic-slice_fusion.2
  9.7 2.3 constant_dynamic-slice_fusion.3
  12.7 11.7 %all_to_all.14 = s32[4,1,4]{2,1,0:T(1,128)S(1)} all-to-all(s32[4,1,4]{2,1,0:T(1,128)S(1)} %bitcast.50), channel_id=1, replica_groups=mesh['groups'=2,'seq'=4,'head'=4] {'seq'}, dimensions={0} | all-to-all | bytes 128 | tf_op jit(solution)/shard_map/all_to_all | solution.py:45
  24.4 0.5 broadcast.146
  24.9 0.7 reduce.3
  25.7 2.8 gather_fusion
  28.5 4.6 broadcast_select_fusion
  33.1 4.8 all-to-all-start.1
  38.2 160.2 %all-to-all-done.1 = bf16[4,4,128,1024]{3,2,1,0:T(8,128)(2,1)} async-done(((bf16[4,4,128,1024]{3,2,1,0:T(8,128)(2,1)}), bf16[4,4,128,1024]{3,2,1,0:T(8,128)(2,1)}, u32[]{:S(2)}, u32[]{:S(2)}) %all-to-all-start.1) | async-done | bytes 4194336 | tf_op jit(solution)/shard_map/all_to_all | solution.py:51
  198.4 2.9 gather_fusion.1
  201.3 1.6 broadcast_select_fusion.1
  203.0 1.5 copy-done.3
  204.5 1.0 constant_dynamic-slice_fusion.1
  205.6 2.3 constant_dynamic-slice_fusion
  208.0 2.2 fusion.1
  210.3 21.7 %all-gather.14.cloned.1.call-done = bf16[4096,1024]{1,0:T(8,128)(2,1)} async-done(((bf16[512,1024]{1,0:T(8,128)(2,1)}), bf16[4096,1024]{1,0:T(8,128)(2,1)}) %all-gather.14.cloned.1.call-update) | async-done | bytes 8388624 | tf_op jit(solution)/shard_map/all_gather | solution.py:13
  232.0 5.8 fusion.21
  237.9 120.3 %all-gather.10.cloned.1.call-done = bf16[4096,1024]{1,0:T(8,128)(2,1)} async-done(((bf16[512,1024]{1,0:T(8,128)(2,1)}), bf16[4096,1024]{1,0:T(8,128)(2,1)}) %all-gather.10.cloned.1.call-update) | async-done | bytes 8388624 | tf_op jit(solution)/shard_map/all_gather | solution.py:13
  358.2 57.9 %all-gather.8.cloned.1.call-done = bf16[8,128,4096]{2,1,0:T(8,128)(2,1)} async-done(((bf16[8,128,1024]{2,1,0:T(8,128)(2,1)}), bf16[8,128,4096]{2,1,0:T(8,128)(2,1)}) %all-gather.8.cloned.1.call-update) | async-done | bytes 8388624 | tf_op jit(solution)/shard_map/all_gather | solution.py:58
  416.1 13.7 %convert_bitcast_fusion.1 = bf16[128,8,8,128]{3,1,2,0:T(8,128)(2,1)S(1)} fusion(bf16[1024,4096]{1,0:T(8,128)(2,1)} %bitcast.51, bf16[4096,1024]{1,0:T(8,128)(2,1)} %all-gather.10.cloned.1.call-done), kind=kOutput, calls=%fused_computation.19 | convolution fusion | flops 8590983168 | bytes 18874368 | tf_op jit(solution)/shard_map/dot_general | solution.py:61
  429.7 2.0 copy.41
  431.7 111.3 %all-gather.16.cloned.1.call-done = bf16[4096,1024]{1,0:T(8,128)(2,1)} async-done(((bf16[512,1024]{1,0:T(8,128)(2,1)}), bf16[4096,1024]{1,0:T(8,128)(2,1)}) %all-gather.16.cloned.1.call-update) | async-done | bytes 8388624 | tf_op jit(solution)/shard_map/all_gather | solution.py:13
  543.0 13.9 %convert_bitcast_fusion = bf16[128,8,8,128]{3,1,2,0:T(8,128)(2,1)S(1)} fusion(bf16[1024,4096]{1,0:T(8,128)(2,1)} %bitcast.52, bf16[4096,1024]{1,0:T(8,128)(2,1)} %all-gather.16.cloned.1.call-done), kind=kOutput, calls=%fused_computation.16 | convolution fusion | flops 8590983168 | bytes 18874368 | tf_op jit(solution)/shard_map/dot_general | solution.py:60
  556.9 0.6 copy.40
  557.5 0.8 fusion.8
  558.4 0.6 fusion.33
  559.0 5.2 fusion.24
  564.6 0.9 copy.54
  565.5 102.6 %all-gather.20.cloned.1.call-done = bf16[4096,1024]{1,0:T(8,128)(2,1)} async-done(((bf16[512,1024]{1,0:T(8,128)(2,1)}), bf16[4096,1024]{1,0:T(8,128)(2,1)}) %all-gather.20.cloned.1.call-update) | async-done | bytes 8388624 | tf_op jit(solution)/shard_map/all_gather | solution.py:13
  668.2 22.4 %all-gather.18.cloned.1.call-done = bf16[256,4096]{1,0:T(8,128)(2,1)} async-done(((bf16[256,1024]{1,0:T(8,128)(2,1)}), bf16[256,4096]{1,0:T(8,128)(2,1)}) %all-gather.18.cloned.1.call-update) | async-done | bytes 2097168 | tf_op jit(solution)/shard_map/all_gather | solution.py:74
  690.5 7.3 %convolution_convert_fusion = bf16[256,1024]{1,0:T(8,128)(2,1)} fusion(bf16[256,4096]{1,0:T(8,128)(2,1)} %all-gather.18.cloned.1.call-done, bf16[4096,1024]{1,0:T(8,128)(2,1)} %all-gather.20.cloned.1.call-done), kind=kOutput, calls=%fused_computation.23 | convolution fusion | flops 2147745792 | bytes 11010048 | tf_op jit(solution)/shard_map/dot_general | solution.py:73
  (47 shorter events, 1.9 us)
Async XLA Ops:
  6.5 19.1 %copy-start = (bf16[8,128,1024]{2,1,0:T(8,128)(2,1)S(1)}, bf16[8,128,1024]{2,1,0:T(8,128)(2,1)}, u32[]{:S(2)}) copy-start(bf16[8,128,1024]{2,1,0:T(8,128)(2,1)} %param.15) | copy-start | bytes 6291460
  6.5 201.5 %all-gather.12.cloned.1.call-start = ((), (), s32[]{:S(2)}) async-start(), calls=%async_computation.4 | async-start | bytes 2621440 | tf_op jit(solution)/shard_map/all_gather | solution.py:17
  7.3 224.7 %all-gather.14.cloned.1.call-start = ((), (), s32[]{:S(2)}) async-start(), calls=%async_computation.5 | async-start | bytes 9437184 | tf_op jit(solution)/shard_map/all_gather | solution.py:13
  9.6 2.4 copy-start.5
  9.6 2.6 copy-start.4
  9.6 348.5 %all-gather.10.cloned.1.call-start = ((), (), s32[]{:S(2)}) async-start(), calls=%async_computation.3 | async-start | bytes 9437184 | tf_op jit(solution)/shard_map/all_gather | solution.py:13
  33.1 165.3 %all-to-all-start.1 = ((bf16[4,4,128,1024]{3,2,1,0:T(8,128)(2,1)}), bf16[4,4,128,1024]{3,2,1,0:T(8,128)(2,1)}, u32[]{:S(2)}, u32[]{:S(2)}) async-start(bf16[4,4,128,1024]{3,2,1,0:T(8,128)(2,1)} %broadcast_select_fusion), calls=%async_computation.1 | async-start | bytes 8388608 | tf_op jit(solution)/shard_map/all_to_all | solution.py:51
  37.9 378.1 %all-gather.8.cloned.1.call-start = ((), (), s32[]{:S(2)}) async-start(), calls=%async_computation.2 | async-start | bytes 10485760 | tf_op jit(solution)/shard_map/all_gather | solution.py:58
  202.9 1.6 copy-start.3
  202.9 340.1 %all-gather.16.cloned.1.call-start = ((), (), s32[]{:S(2)}) async-start(), calls=%async_computation.6 | async-start | bytes 9437184 | tf_op jit(solution)/shard_map/all_gather | solution.py:13
  205.5 462.6 %all-gather.20.cloned.1.call-start = ((), (), s32[]{:S(2)}) async-start(), calls=%async_computation.8 | async-start | bytes 9437184 | tf_op jit(solution)/shard_map/all_gather | solution.py:13
  207.9 24.1 %copy-start.6 = (f32[4096]{0:T(1024)S(1)}, f32[4096]{0:T(1024)}, u32[]{:S(2)}) copy-start(f32[4096]{0:T(1024)} %param.10) | copy-start | bytes 49156
  207.9 482.6 %all-gather.18.cloned.1.call-start = ((), (), s32[]{:S(2)}) async-start(), calls=%async_computation.7 | async-start | bytes 2621440 | tf_op jit(solution)/shard_map/all_gather | solution.py:74
  208.0 24.0 %copy-start.2 = (bf16[256,4096]{1,0:T(8,128)(2,1)S(1)}, bf16[256,4096]{1,0:T(8,128)(2,1)}, u32[]{:S(2)}) copy-start(bf16[256,4096]{1,0:T(8,128)(2,1)} %all-gather.12.cloned.1.call-done) | copy-start | bytes 6291460
  690.5 7.3 %copy-start.1 = (bf16[8,128,1024]{2,1,0:T(8,128)(2,1)S(1)}, bf16[8,128,1024]{2,1,0:T(8,128)(2,1)}, u32[]{:S(2)}) copy-start(bf16[8,128,1024]{2,1,0:T(8,128)(2,1)} %param.15) | copy-start | bytes 6291460
Sparse Core Ops, SparseCore 0:
  8.9 25.2 all-gather.11
  36.4 195.5 all-gather.13
  234.1 123.9 all-gather.9
  359.6 56.4 all-gather.7
  418.0 124.9 all-gather.15
  545.0 123.1 all-gather.19
  669.7 20.7 all-gather.17

commit v2 on v0

v2 whole, which is shorter than its diff:
```python
import jax
import jax.numpy as jnp
from jax import lax
from jax.sharding import PartitionSpec as P

HD = 128


def column_half(weight):
    cols = weight.shape[1] // 2
    return lax.dynamic_slice_in_dim(weight, lax.axis_index("groups") * cols, cols, axis=1)


def gather_halves(weight):
    mine = lax.all_gather(column_half(weight), "seq", axis=0, tiled=True)
    other = lax.ppermute(mine, "groups", [(0, 1), (1, 0)])
    return mine, other


def project(rows, halves):
    mine, other = (jnp.dot(rows, half, preferred_element_type=jnp.float32) for half in halves)
    first = lax.axis_index("groups") == 0
    return jnp.concatenate([jnp.where(first, mine, other), jnp.where(first, other, mine)], axis=1)


def normalize(tokens, norm_gain):
    x = tokens.astype(jnp.float32)
    feat_dev = tokens.shape[1]
    total = lax.psum(jnp.sum(x * x, axis=-1, keepdims=True), "head")
    inverse = lax.rsqrt(total / (feat_dev * lax.axis_size("head")) + 1e-06)
    gain = lax.dynamic_slice_in_dim(norm_gain, lax.axis_index("head") * feat_dev, feat_dev)
    return (x * inverse * gain).astype(jnp.bfloat16)


def every_query(normed, w_query):
    scale = jnp.sqrt(jnp.float32(HD))
    num = lax.axis_size("seq")
    if num == lax.axis_size("head"):
        swap = [(a * num + b, b * num + a) for a in range(num) for b in range(num)]
        turned = lax.ppermute(normed, ("seq", "head"), swap)
        rows = lax.all_gather(turned, "head", axis=0, tiled=True)
        part = jnp.dot(rows, w_query, preferred_element_type=jnp.float32) / scale
        return lax.psum(part.astype(jnp.bfloat16), "seq")
    rows = lax.all_gather(normed, "head", axis=1, tiled=True)
    query = jnp.dot(
        rows,
        lax.all_gather(w_query, "seq", axis=0, tiled=True),
        preferred_element_type=jnp.float32,
    )
    return lax.all_gather((query / scale).astype(jnp.bfloat16), "seq", axis=0, tiled=True)


def local(tokens, norm_gain, w_query, w_key, w_value, w_out, database, nbr_shard, nbr_row):
    key_halves = gather_halves(w_key)
    value_halves = gather_halves(w_value)
    out_halves = gather_halves(w_out)
    rows_dev, ntok, _ = database.shape
    flat = lax.all_gather(database, "head", axis=2, tiled=True).reshape(rows_dev * ntok, -1)
    query = every_query(normalize(tokens, norm_gain), w_query)

    me = lax.axis_index("seq")
    near = lax.all_gather(jnp.concatenate([nbr_shard, nbr_row], axis=1), "seq", axis=0, tiled=True)
    here = near[:, :2] == me
    mine = jnp.any(here, axis=1)
    row = jnp.sum(jnp.where(here, near[:, 2:], 0), axis=1)

    spans = near.shape[0]
    width = w_key.shape[1]
    heads_dev = width // HD
    span_len = query.shape[0] // spans
    keys = project(flat, key_halves).astype(jnp.bfloat16).reshape(rows_dev, ntok, width)
    values = project(flat, value_halves).astype(jnp.bfloat16).reshape(rows_dev, ntok, width)
    keys = jnp.take(keys, row, axis=0).reshape(spans, ntok, heads_dev, HD)
    values = jnp.take(values, row, axis=0).reshape(spans, ntok, heads_dev, HD)
    qh = query.reshape(spans, span_len, heads_dev, HD)
    scores = jnp.einsum("cqhd,ckhd->chqk", qh, keys, preferred_element_type=jnp.float32)
    scores = jnp.where(mine[:, None, None, None], scores, -jnp.inf)
    top = jnp.max(scores, axis=-1)
    summed = jnp.sum(jnp.exp(scores - jnp.where(jnp.isfinite(top), top, 0.0)[..., None]), axis=-1)
    tops, sums = lax.all_gather(jnp.stack([top, summed]), "seq", axis=1)
    most = jnp.max(tops, axis=0)
    denominator = jnp.sum(jnp.exp(tops - most) * sums, axis=0)
    weights = (jnp.exp(scores - most[..., None]) / denominator[..., None]).astype(jnp.bfloat16)
    context = jnp.einsum("chqk,ckhd->cqhd", weights, values, preferred_element_type=jnp.float32)
    context = context.astype(jnp.bfloat16).reshape(spans * span_len, width)
    context = lax.psum_scatter(context, "seq", scatter_dimension=0, tiled=True)
    attended = project(lax.all_gather(context, "head", axis=1, tiled=True), out_halves)
    return attended.astype(jnp.bfloat16)


def solution(mesh):
    return jax.shard_map(
        local,
        mesh=mesh,
        in_specs=(
            P(("groups", "seq"), "head"),
            P(),
            P("seq", "head"),
            P("seq", "head"),
            P("seq", "head"),
            P("seq", "head"),
            P(("groups", "seq"), None, "head"),
            P(("groups", "seq"), None),
            P(("groups", "seq"), None),
        ),
        out_specs=P(("groups", "seq"), "head"),
        check_vma=False,
    )
```

time: 808 us -> 572 us (0.71)
  waiting for transfers between devices: 709 us -> 398 us
  blocking collectives: 11.7 us -> 42.2 us
  local copies, waits for them, and re-layouts: 10.8 us -> 39.9 us
  matrix products: 46.7 us -> 55.2 us
    all_to_all x1 -> x0, waiting for transfers between devices: 199 us -> none  [local(): lax.all_to_all(outgoing, 'seq', split_axis=0, concat_axis=0, tiled=True)]
    all_gather x6 -> x5, waiting for transfers between devices: 485 us -> 290 us  [the longest x3 190 us: gather_halves(): mine = lax.all_gather(column_half(weight), 'seq', axis=0, tiled=True)]
    reduce_scatter x0 -> x1, waiting for transfers between devices: none -> 44.4 us  [local(): context = lax.psum_scatter(context, 'seq', scatter_dimension=0, tiled=True)]
    ppermute x0 -> x4, waiting for transfers between devices: none -> 35 us  [the longest x3 35 us: gather_halves(): other = lax.ppermute(mine, 'groups', [(0, 1), (1, 0)])]
    all_gather x0 -> x2, blocking collectives: none -> 33.9 us  [the longest x1 21.7 us: local(): tops, sums = lax.all_gather(jnp.stack([top, summed]), 'seq', axis=1)]
    select_n x0 -> x2, local copies, waits for them, and re-layouts: none -> 12.7 us  [the longest x1 6.41 us: local(): values = jnp.take(values, row, axis=0).reshape(spans, ntok, heads_dev, HD)]
    all_to_all x1 -> x0, blocking collectives: 11.7 us -> none  [local(): lax.all_to_all(wanted, 'seq', split_axis=0, concat_axis=0, tiled=True)]
    psum x0 -> x1, blocking collectives: none -> 8.34 us  [normalize(): total = lax.psum(jnp.sum(x * x, axis=-1, keepdims=True), 'head')]
  transfers between devices with their start and end apart: 8 -> 12, of which waited for: 7 -> 10; matrix products, arithmetic and copies ran while one was open for 7% -> 18% of each run, Pallas kernels for 0% -> 0%
where the time goes in v2:
time: 572 us; the launch traced here: 571 us
  waiting for transfers between devices  398 us (70%)
  matrix products  55.2 us (10%)
  blocking collectives  42.2 us (7%)
  local copies, waits for them, and re-layouts  39.9 us (7%)
  other arithmetic  16.5 us (3%)
  between operations  13.8 us (2%)
    all_gather x3, waiting for transfers between devices, gather_halves(): mine = lax.all_gather(column_half(weight), 'seq', axis=0, tiled=True)  190 us
    all_gather x1, waiting for transfers between devices, local(): lax.all_gather(database, 'head', axis=2, tiled=True)  56.6 us
    reduce_scatter x1, waiting for transfers between devices, local(): context = lax.psum_scatter(context, 'seq', scatter_dimension=0, tiled=True)  44.4 us
    all_gather x1, waiting for transfers between devices, every_query(): rows = lax.all_gather(turned, 'head', axis=0, tiled=True)  43.4 us
    dot_general x6, matrix products, project(): jnp.dot(rows, half, preferred_element_type=jnp.float32)  42.2 us
    ppermute x3, waiting for transfers between devices, gather_halves(): other = lax.ppermute(mine, 'groups', [(0, 1), (1, 0)])  35 us
    all_gather x1, waiting for transfers between devices, local(): lax.all_gather(context, 'head', axis=1, tiled=True)  23.5 us
    all_gather x1, blocking collectives, local(): tops, sums = lax.all_gather(jnp.stack([top, summed]), 'seq', axis=1)  21.7 us
  transfers between devices with their start and end apart: 12, of which 10 were waited for; matrix products, arithmetic and copies ran while one was open for 18% of the time, Pallas kernels for 0%

profile of v2, /device:TPU:0, one launch (start us, length us, event | category | flops | bytes accessed | tf_op | source)
XLA Modules:
  0.0 571.3 jit_solution(9789028276854825734)
XLA Ops:
  7.9 8.3 %psum.14 = f32[256,1]{0,1:T(1,128)S(1)} all-reduce(f32[256,1]{0,1:T(1,128)S(1)} %bitcast.68), channel_id=1, replica_groups=mesh['groups'=2,'seq'=4,'head'=4] {'head'}, use_global_device_ids=true, to_apply=%region_3.5 | all-reduce | flops 256 | bytes 2048 | tf_op jit(solution)/shard_map/psum | solution.py:29
  19.8 2.3 constant_dynamic-slice_fusion.2
  22.1 2.3 constant_dynamic-slice_fusion.1
  25.1 43.4 %all-gather.13.cloned.1.call-done = bf16[1024,1024]{1,0:T(8,128)(2,1)} async-done(((bf16[256,1024]{1,0:T(8,128)(2,1)}), bf16[1024,1024]{1,0:T(8,128)(2,1)}) %all-gather.13.cloned.1.call-update) | async-done | bytes 2097168 | tf_op jit(solution)/shard_map/all_gather | solution.py:41
  68.5 3.9 fusion.5
  75.0 75.8 %all-gather.9.cloned.1.call-done = bf16[4096,512]{1,0:T(8,128)(2,1)} async-done(((bf16[1024,512]{1,0:T(8,128)(2,1)}), bf16[4096,512]{1,0:T(8,128)(2,1)}) %all-gather.9.cloned.1.call-update) | async-done | bytes 4194320 | tf_op jit(solution)/shard_map/all_gather | solution.py:15
  152.4 2.3 constant_dynamic-slice_fusion
  154.9 12.2 %all-gather.1 = s32[4,4,4]{2,1,0:T(4,128)S(1)} all-gather(s32[1,4,4]{2,1,0:T(4,128)S(1)} %bitcast.66), channel_id=1, replica_groups=mesh['groups'=2,'seq'=4,'head'=4] {'seq'}, dimensions={0}, use_global_device_ids=true | all-gather | bytes 320 | tf_op jit(solution)/shard_map/all_gather | solution.py:62
  167.2 64.6 %all-gather.15.cloned.1.call-done = bf16[4096,512]{1,0:T(8,128)(2,1)} async-done(((bf16[1024,512]{1,0:T(8,128)(2,1)}), bf16[4096,512]{1,0:T(8,128)(2,1)}) %all-gather.15.cloned.1.call-update) | async-done | bytes 4194320 | tf_op jit(solution)/shard_map/all_gather | solution.py:15
  233.5 56.6 %all-gather.11.cloned.1.call-done = bf16[8,128,4096]{2,1,0:T(8,128)(2,1)} async-done(((bf16[8,128,1024]{2,1,0:T(8,128)(2,1)}), bf16[8,128,4096]{2,1,0:T(8,128)(2,1)}) %all-gather.11.cloned.1.call-update) | async-done | bytes 8388624 | tf_op jit(solution)/shard_map/all_gather | solution.py:58
  290.1 9.3 %fusion.17 = bf16[512,1024]{1,0:T(8,128)(2,1)S(1)} fusion(bf16[4096,512]{1,0:T(8,128)(2,1)} %all-gather.9.cloned.1.call-done, bf16[1024,4096]{1,0:T(8,128)(2,1)} %bitcast.69), kind=kOutput, calls=%fused_computation.51 | convolution fusion | flops 4294967296 | bytes 13631488 | tf_op jit(solution)/shard_map/dot_general | solution.py:21
  299.4 6.7 %fusion.9 = (bf16[1024,512]{0,1:T(8,128)(2,1)S(1)}, bf16[1024,512]{0,1:T(8,128)(2,1)S(1)}) fusion(bf16[512,1024]{1,0:T(8,128)(2,1)S(1)} %fusion.17, pred[]{:T(512)S(6)} %eq.11, bf16[4096,512]{1,0:T(8,128)(2,1)} %collective-permute-done, bf16[1024,4096]{1,0:T(8,128)(2,1)S(1)} %bitcast.72), kind=kOutput, calls=%fused_computation.27 | convolution fusion | flops 4296015872 | bytes 15728641 | tf_op jit(solution)/shard_map/dot_general | solution.py:21
  308.3 9.3 %fusion.18 = bf16[512,1024]{1,0:T(8,128)(2,1)S(1)} fusion(bf16[4096,512]{1,0:T(8,128)(2,1)} %all-gather.15.cloned.1.call-done, bf16[1024,4096]{1,0:T(8,128)(2,1)} %bitcast.70), kind=kOutput, calls=%fused_computation.52 | convolution fusion | flops 4294967296 | bytes 13631488 | tf_op jit(solution)/shard_map/dot_general | solution.py:21
  317.5 15.9 %collective-permute-done.2 = bf16[4096,512]{1,0:T(8,128)(2,1)} collective-permute-done((bf16[4096,512]{1,0:T(8,128)(2,1)}, bf16[4096,512]{1,0:T(8,128)(2,1)}, u32[]{:S(2)}, u32[]{:S(2)}) %collective-permute-start.2) | collective-permute-done | bytes 4194336 | tf_op jit(solution)/shard_map/ppermute | solution.py:16
  333.4 9.2 %fusion.11 = (bf16[1024,512]{0,1:T(8,128)(2,1)S(1)}, bf16[1024,512]{0,1:T(8,128)(2,1)S(1)}) fusion(bf16[512,1024]{1,0:T(8,128)(2,1)S(1)} %fusion.18, pred[]{:T(512)S(6)} %eq.11, bf16[4096,512]{1,0:T(8,128)(2,1)} %collective-permute-done.2, bf16[1024,4096]{1,0:T(8,128)(2,1)} %bitcast.71), kind=kOutput, calls=%fused_computation.29 | convolution fusion | flops 4296015872 | bytes 15728641 | tf_op jit(solution)/shard_map/dot_general | solution.py:21
  346.8 2.8 gather_fusion
  351.0 2.8 gather_fusion.1
  353.8 7.5 %broadcast_select_fusion = (bf16[16,128,1024]{2,1,0:T(8,128)(2,1)}, bf16[16,128,1024]{2,1,0:T(8,128)(2,1)}) fusion(bf16[16,128,1024]{2,1,0:T(8,128)(2,1)} %gather_fusion.1, pred[16]{0:T(512)(128)(4,1)S(1)} %compare_and_fusion, bf16[16,128,1024]{2,1,0:T(8,128)(2,1)} %gather_fusion), kind=kLoop, calls=%fused_computation.5 | loop fusion | flops 4194304 | bytes 16777232 | tf_op jit(solution)/shard_map/jit(_take)/select_n | solution.py:73
  361.4 6.3 %copy.33 = bf16[16,128,1024]{1,2,0:T(8,128)(2,1)} copy(bf16[16,128,1024]{2,1,0:T(8,128)(2,1)} %get-tuple-element.16) | data formatting | bytes 8388608 | tf_op jit(solution)/shard_map/jit(_take)/select_n | solution.py:73
  367.7 6.4 %copy.29 = bf16[16,128,1024]{1,2,0:T(8,128)(2,1)} copy(bf16[16,128,1024]{2,1,0:T(8,128)(2,1)} %get-tuple-element.17) | data formatting | bytes 8388608 | tf_op jit(solution)/shard_map/jit(_take)/select_n | solution.py:74
  374.1 4.7 all-reduce.2.cloned.1.call-done
  378.8 4.1 select_reduce_fusion
  384.9 2.4 exponential_reduce_fusion
  387.3 21.7 %all-gather = f32[2,64,8,64]{3,2,1,0:T(8,128)S(1)} all-gather(f32[2,16,8,64]{3,2,1,0:T(8,128)S(1)} %pad_maximum_fusion.3), channel_id=2, replica_groups=mesh['groups'=2,'seq'=4,'head'=4] {'seq'}, dimensions={1}, use_global_device_ids=true | all-gather | bytes 327680 | tf_op jit(solution)/shard_map/all_gather | solution.py:80
  409.1 4.9 convert_bitcast_fusion
  415.8 2.0 copy.49
  417.8 49.5 %all-gather.19.cloned.1.call-done = bf16[4096,512]{1,0:T(8,128)(2,1)} async-done(((bf16[1024,512]{1,0:T(8,128)(2,1)}), bf16[4096,512]{1,0:T(8,128)(2,1)}) %all-gather.19.cloned.1.call-update) | async-done | bytes 4194320 | tf_op jit(solution)/shard_map/all_gather | solution.py:15
  468.8 44.4 %reduce-scatter.2.cloned.1.call-done = bf16[256,1024]{1,0:T(8,128)(2,1)} async-done(((bf16[1024,1024]{1,0:T(8,128)(2,1)}), bf16[256,1024]{1,0:T(8,128)(2,1)}) %reduce-scatter.2.cloned.1.call-update) | async-done | bytes 524304 | tf_op jit(solution)/shard_map/reduce_scatter | solution.py:86
  513.3 23.5 %all-gather.17.cloned.1.call-done = bf16[256,4096]{1,0:T(8,128)(2,1)} async-done(((bf16[256,1024]{1,0:T(8,128)(2,1)}), bf16[256,4096]{1,0:T(8,128)(2,1)}) %all-gather.17.cloned.1.call-update) | async-done | bytes 2097168 | tf_op jit(solution)/shard_map/all_gather | solution.py:87
  536.7 4.2 fusion.19
  541.0 19.2 %collective-permute-done.3 = bf16[4096,512]{1,0:T(8,128)(2,1)} collective-permute-done((bf16[4096,512]{1,0:T(8,128)(2,1)}, bf16[4096,512]{1,0:T(8,128)(2,1)}, u32[]{:S(2)}, u32[]{:S(2)}) %collective-permute-start.3) | collective-permute-done | bytes 4194336 | tf_op jit(solution)/shard_map/ppermute | solution.py:16
  560.1 3.5 select_convert_fusion.5
  (69 shorter events, 25.6 us)
Async XLA Ops:
  6.5 62.0 %copy-start = (bf16[1024,1024]{1,0:T(8,128)(2,1)S(1)}, bf16[1024,1024]{1,0:T(8,128)(2,1)}, u32[]{:S(2)}) copy-start(bf16[1024,1024]{1,0:T(8,128)(2,1)} %param.13) | copy-start | bytes 6291460
  6.5 61.9 %all-gather.13.cloned.1.call-start = ((), (), s32[]{:S(2)}) async-start(), calls=%async_computation.3 | async-start | bytes 2621440 | tf_op jit(solution)/shard_map/all_gather | solution.py:41
  18.2 0.7 collective-permute-start.1
  18.9 0.8 copy-start.4
  19.7 131.1 %all-gather.9.cloned.1.call-start = ((), (), s32[]{:S(2)}) async-start(), calls=%async_computation.1 | async-start | bytes 5242880 | tf_op jit(solution)/shard_map/all_gather | solution.py:15
  22.1 209.7 %all-gather.15.cloned.1.call-start = ((), (), s32[]{:S(2)}) async-start(), calls=%async_computation.5 | async-start | bytes 5242880 | tf_op jit(solution)/shard_map/all_gather | solution.py:15
  24.4 265.6 %all-gather.11.cloned.1.call-start = ((), (), s32[]{:S(2)}) async-start(), calls=%async_computation.2 | async-start | bytes 10485760 | tf_op jit(solution)/shard_map/all_gather | solution.py:58
  25.0 353.8 %all-reduce.2.cloned.1.call-start = ((), (), s32[]{:S(2)}) async-start(), calls=%async_computation.4 | async-start | bytes 4194304 | tf_op jit(solution)/shard_map/psum | solution.py:43
  73.0 81.7 %copy-start.5 = (s32[4,2]{0,1:T(2,128)S(1)}, s32[4,2]{0,1:T(2,128)}, u32[]{:S(2)}) copy-start(s32[4,2]{0,1:T(2,128)} %param.19) | copy-start | bytes 100
  73.1 81.7 %copy-start.6 = (s32[4,2]{0,1:T(2,128)S(1)}, s32[4,2]{0,1:T(2,128)}, u32[]{:S(2)}) copy-start(s32[4,2]{0,1:T(2,128)} %param.18) | copy-start | bytes 100
  75.0 392.4 %all-gather.19.cloned.1.call-start = ((), (), s32[]{:S(2)}) async-start(), calls=%async_computation.8 | async-start | bytes 5242880 | tf_op jit(solution)/shard_map/all_gather | solution.py:15
  150.9 148.5 %collective-permute-start = (bf16[4096,512]{1,0:T(8,128)(2,1)}, bf16[4096,512]{1,0:T(8,128)(2,1)}, u32[]{:S(2)}, u32[]{:S(2)}) collective-permute-start(bf16[4096,512]{1,0:T(8,128)(2,1)} %all-gather.9.cloned.1.call-done), channel_id=1, source_target_pairs={{0,16},{16,0},{1,17},{17,1},{2,18},{18,2},{3,19},{19,3},{4,20},{20... | collective-permute-start | bytes 12582920 | tf_op jit(solution)/shard_map/ppermute | solution.py:16
  154.7 358.6 %reduce-scatter.2.cloned.1.call-start = ((), (), s32[]{:S(2)}) async-start(), calls=%async_computation.6 | async-start | bytes 2621440 | tf_op jit(solution)/shard_map/reduce_scatter | solution.py:86
  231.8 101.6 %collective-permute-start.2 = (bf16[4096,512]{1,0:T(8,128)(2,1)}, bf16[4096,512]{1,0:T(8,128)(2,1)}, u32[]{:S(2)}, u32[]{:S(2)}) collective-permute-start(bf16[4096,512]{1,0:T(8,128)(2,1)} %all-gather.15.cloned.1.call-done), channel_id=1, source_target_pairs={{0,16},{16,0},{1,17},{17,1},{2,18},{18,2},{3,19},{19,3},{4,20},{20... | collective-permute-start | bytes 12582920 | tf_op jit(solution)/shard_map/ppermute | solution.py:16
  290.0 9.4 %copy-start.7 = (bf16[8,128,4096]{2,1,0:T(8,128)(2,1)S(1)}, bf16[8,128,4096]{2,1,0:T(8,128)(2,1)}, u32[]{:S(2)}) copy-start(bf16[8,128,4096]{2,1,0:T(8,128)(2,1)} %all-gather.11.cloned.1.call-done) | copy-start | bytes 25165828
  346.8 2.8 copy-start.3
  383.0 1.9 copy-start.2
  417.8 118.9 %all-gather.17.cloned.1.call-start = ((), (), s32[]{:S(2)}) async-start(), calls=%async_computation.7 | async-start | bytes 2621440 | tf_op jit(solution)/shard_map/all_gather | solution.py:87
  467.4 92.8 %collective-permute-start.3 = (bf16[4096,512]{1,0:T(8,128)(2,1)}, bf16[4096,512]{1,0:T(8,128)(2,1)}, u32[]{:S(2)}, u32[]{:S(2)}) collective-permute-start(bf16[4096,512]{1,0:T(8,128)(2,1)} %all-gather.19.cloned.1.call-done), channel_id=1, source_target_pairs={{0,16},{16,0},{1,17},{17,1},{2,18},{18,2},{3,19},{19,3},{4,20},{20... | collective-permute-start | bytes 12582920 | tf_op jit(solution)/shard_map/ppermute | solution.py:16
  536.7 23.4 %copy-start.8 = (bf16[256,4096]{1,0:T(8,128)(2,1)S(1)}, bf16[256,4096]{1,0:T(8,128)(2,1)}, u32[]{:S(2)}) copy-start(bf16[256,4096]{1,0:T(8,128)(2,1)} %all-gather.17.cloned.1.call-done) | copy-start | bytes 6291460
  536.7 27.7 %copy-start.1 = (bf16[1024,1024]{1,0:T(8,128)(2,1)S(1)}, bf16[1024,1024]{1,0:T(8,128)(2,1)}, u32[]{:S(2)}) copy-start(bf16[1024,1024]{1,0:T(8,128)(2,1)} %param.13) | copy-start | bytes 6291460
Sparse Core Ops, SparseCore 0:
  19.8 48.5 all-gather.12
  70.1 80.7 all-gather.8
  152.4 79.2 all-gather.14
  233.2 56.8 all-gather.10
  292.3 86.5 all-reduce.1
  380.3 86.9 all-gather.18
  469.7 43.4 reduce-scatter.1
  514.8 21.8 all-gather.16

commit v3 on v2

--- a/solution.py
+++ b/solution.py
@@ -1,6 +1,10 @@
+import functools
+
 import jax
 import jax.numpy as jnp
 from jax import lax
+from jax.experimental import pallas as pl
+from jax.experimental.pallas import tpu as pltpu
 from jax.sharding import PartitionSpec as P
 
 HD = 128
@@ -32,7 +36,7 @@
     return (x * inverse * gain).astype(jnp.bfloat16)
 
 
-def every_query(normed, w_query):
+def partial_query(normed, w_query):
     scale = jnp.sqrt(jnp.float32(HD))
     num = lax.axis_size("seq")
     if num == lax.axis_size("head"):
@@ -40,23 +44,240 @@
         turned = lax.ppermute(normed, ("seq", "head"), swap)
         rows = lax.all_gather(turned, "head", axis=0, tiled=True)
         part = jnp.dot(rows, w_query, preferred_element_type=jnp.float32) / scale
-        return lax.psum(part.astype(jnp.bfloat16), "seq")
+        return part.astype(jnp.bfloat16)
     rows = lax.all_gather(normed, "head", axis=1, tiled=True)
     query = jnp.dot(
         rows,
         lax.all_gather(w_query, "seq", axis=0, tiled=True),
         preferred_element_type=jnp.float32,
     )
-    return lax.all_gather((query / scale).astype(jnp.bfloat16), "seq", axis=0, tiled=True)
+    return (query / scale).astype(jnp.bfloat16)
+
+
+def whole_query(part):
+    if lax.axis_size("seq") == lax.axis_size("head"):
+        return lax.psum(part, "seq")
+    return lax.all_gather(part, "seq", axis=0, tiled=True)
+
+
+MESH = pl.DeviceIdType.MESH
+
+
+def project_kernel(
+    n_seq, n_head, database, w_key, w_value, keys, values, whole, held, total,
+    near_send, near_recv, side_send, side_recv, row_send, row_recv, row_copy,
+):
+    g, z, h = lax.axis_index("groups"), lax.axis_index("seq"), lax.axis_index("head")
+    weights = (w_key, w_value)
+    depth, width = w_key.shape
+    half = depth // 2
+    feats = database.shape[1]
+    tile = min(256, width)
+
+    barrier = pltpu.get_barrier_semaphore()
+
+    def greet(**where):
+        pl.semaphore_signal(barrier, inc=1, device_id=where, device_id_type=MESH)
+
+    @pl.when(z > 0)
+    def _():
+        greet(seq=z - 1)
+
+    @pl.when(z < n_seq - 1)
+    def _():
+        greet(seq=z + 1)
+
+    greet(groups=1 - g)
+    for step in range(1, n_head):
+        greet(head=lax.rem(h + step, n_head))
+
+    ends = jnp.where(z > 0, 0, 1) + jnp.where(z < n_seq - 1, 0, 1)
+    pl.semaphore_wait(barrier, n_head + 2 - ends)
+
+    def span(owner, part):
+        return pl.ds(pl.multiple_of(owner * depth + part * half, half), half)
+
+    def along(w, owner, way, own=False):
+        source = held.at[w, span(owner, g)]
+        if own:
+            source = weights[w].at[pl.ds(pl.multiple_of(g * half, half), half)]
+        return pltpu.make_async_remote_copy(
+            src_ref=source,
+            dst_ref=held.at[w, span(owner, g)],
+            send_sem=near_send.at[w, owner, way],
+            recv_sem=near_recv.at[w, owner],
+            device_id={"seq": z + 1 - 2 * way},
+            device_id_type=MESH,
+        )
+
+    def across(w, owner, part):
+        return pltpu.make_async_remote_copy(
+            src_ref=held.at[w, span(owner, part)],
+            dst_ref=held.at[w, span(owner, part)],
+            send_sem=side_send.at[w, owner],
+            recv_sem=side_recv.at[w, owner],
+            device_id={"groups": 1 - g},
+            device_id_type=MESH,
+        )
+
+    def columns(source):
+        return pl.ds(pl.multiple_of(source * feats, feats), feats)
+
+    def row_move(source, target):
+        return pltpu.make_async_remote_copy(
+            src_ref=database,
+            dst_ref=whole.at[:, columns(source)],
+            send_sem=row_send.at[target],
+            recv_sem=row_recv.at[source],
+            device_id={"head": target},
+            device_id_type=MESH,
+        )
+
+    for w in range(2):
+
+        @pl.when(z < n_seq - 1)
+        def _():
+            along(w, z, 0, own=True).start()
+
+        @pl.when(z > 0)
+        def _():
+            along(w, z, 1, own=True).start()
+
+    for step in range(1, n_head):
+        row_move(h, lax.rem(h + step, n_head)).start()
+    keep = pltpu.make_async_copy(database, whole.at[:, columns(h)], row_copy)
+    keep.start()
+
+    def valid(d, way):
+        return z - d >= 0 if way == 0 else z + d < n_seq
+
+    def owner_of(d, way):
+        return z - d if way == 0 else z + d
+
+    def forward(d):
+        for w in range(2):
+            for way in range(2):
+                owner = owner_of(d, way)
+
+                @pl.when(valid(d, way))
+                def _():
+                    along(w, owner, way).wait_recv()
+                    across(w, owner, g).start()
+
+                    @pl.when(z < n_seq - 1 if way == 0 else z > 0)
+                    def _():
+                        along(w, owner, way).start()
+
+    def add(w, owner, block, first=False):
+        left = whole.at[:, pl.ds(pl.multiple_of(owner * depth, depth), depth)]
+
+        def body(t, carry):
+            at = pl.ds(pl.multiple_of(t * tile, tile), tile)
+            term = jnp.dot(left[...], block[:, at], preferred_element_type=jnp.float32)
+            if first:
+                total[w, :, at] = term
+            else:
+                total[w, :, at] += term
+            return carry
+
+        lax.fori_loop(0, width // tile, body, 0)
+
+    def multiply(d):
+        for w in range(2):
+            for way in range(2):
+                owner = owner_of(d, way)
+
+                @pl.when(valid(d, way))
+                def _():
+                    across(w, owner, 1 - g).wait_recv()
+                    add(w, owner, held.at[w, pl.ds(pl.multiple_of(owner * depth, depth), depth)])
+
+    early = min(2, n_seq - 1)
+    for d in range(1, early + 1):
+        forward(d)
+    keep.wait()
+    for step in range(1, n_head):
+        source = lax.rem(h + step, n_head)
+        row_move(source, source).wait_recv()
+    for w in range(2):
+        add(w, z, weights[w], first=True)
+    for d in range(1, n_seq):
+        if d > early:
+            forward(d)
+        if d < n_seq - 1:
+            multiply(d)
+    if n_seq > 1:
+        multiply(n_seq - 1)
+
+    keys[...] = total[0].astype(keys.dtype)
+    values[...] = total[1].astype(values.dtype)
+
+    for step in range(1, n_head):
+        row_move(h, lax.rem(h + step, n_head)).wait_send()
+    for w in range(2):
+
+        @pl.when(z < n_seq - 1)
+        def _():
+            along(w, z, 0, own=True).wait_send()
+
+        @pl.when(z > 0)
+        def _():
+            along(w, z, 1, own=True).wait_send()
+
+        for d in range(1, n_seq):
+            for way in range(2):
+                owner = owner_of(d, way)
+
+                @pl.when(valid(d, way))
+                def _():
+                    across(w, owner, g).wait_send()
+
+                    @pl.when(z < n_seq - 1 if way == 0 else z > 0)
+                    def _():
+                        along(w, owner, way).wait_send()
+
+
+def keys_and_values(database, w_key, w_value):
+    n_seq, n_head = lax.axis_size("seq"), lax.axis_size("head")
+    rows, feats = database.shape
+    depth, width = w_key.shape
+    vmem = pl.BlockSpec(memory_space=pltpu.VMEM)
+    return pl.pallas_call(
+        functools.partial(project_kernel, n_seq, n_head),
+        out_shape=[jax.ShapeDtypeStruct((rows, width), jnp.bfloat16)] * 2,
+        in_specs=[pl.BlockSpec(memory_space=pl.ANY), vmem, vmem],
+        out_specs=[vmem, vmem],
+        scratch_shapes=[
+            pltpu.VMEM((rows, feats * n_head), jnp.bfloat16),
+            pltpu.VMEM((2, depth * n_seq, width), jnp.bfloat16),
+            pltpu.VMEM((2, rows, width), jnp.float32),
+            pltpu.SemaphoreType.DMA((2, n_seq, 2)),
+            pltpu.SemaphoreType.DMA((2, n_seq)),
+            pltpu.SemaphoreType.DMA((2, n_seq)),
+            pltpu.SemaphoreType.DMA((2, n_seq)),
+            pltpu.SemaphoreType.DMA((n_head,)),
+            pltpu.SemaphoreType.DMA((n_head,)),
+            pltpu.SemaphoreType.DMA,
+        ],
+        compiler_params=pltpu.CompilerParams(
+            collective_id=0, has_side_effects=True, vmem_limit_bytes=56 * 1024 * 1024
+        ),
+        cost_estimate=pl.CostEstimate(
+            flops=4 * rows * depth * n_seq * width,
+            bytes_accessed=500 * 1024 * 1024,
+            transcendentals=0,
+        ),
+    )(database, w_key, w_value)
 
 
 def local(tokens, norm_gain, w_query, w_key, w_value, w_out, database, nbr_shard, nbr_row):
-    key_halves = gather_halves(w_key)
-    value_halves = gather_halves(w_value)
+    rows_dev, ntok, feat_dev = database.shape
+    part = partial_query(normalize(tokens, norm_gain), w_query)
+    part, w_key, w_value = lax.optimization_barrier((part, w_key, w_value))
+    query = whole_query(part)
+    keys, values = keys_and_values(database.reshape(rows_dev * ntok, feat_dev), w_key, w_value)
+    keys, values, w_out = lax.optimization_barrier((keys, values, w_out))
     out_halves = gather_halves(w_out)
-    rows_dev, ntok, _ = database.shape
-    flat = lax.all_gather(database, "head", axis=2, tiled=True).reshape(rows_dev * ntok, -1)
-    query = every_query(normalize(tokens, norm_gain), w_query)
 
     me = lax.axis_index("seq")
     near = lax.all_gather(jnp.concatenate([nbr_shard, nbr_row], axis=1), "seq", axis=0, tiled=True)
@@ -68,8 +289,8 @@
     width = w_key.shape[1]
     heads_dev = width // HD
     span_len = query.shape[0] // spans
-    keys = project(flat, key_halves).astype(jnp.bfloat16).reshape(rows_dev, ntok, width)
-    values = project(flat, value_halves).astype(jnp.bfloat16).reshape(rows_dev, ntok, width)
+    keys = keys.reshape(rows_dev, ntok, width)
+    values = values.reshape(rows_dev, ntok, width)
     keys = jnp.take(keys, row, axis=0).reshape(spans, ntok, heads_dev, HD)
     values = jnp.take(values, row, axis=0).reshape(spans, ntok, heads_dev, HD)
     qh = query.reshape(spans, span_len, heads_dev, HD)

time: 572 us -> 510 us (0.89)
  waiting for transfers between devices: 398 us -> 147 us
  Pallas kernels: 0 us -> 241 us
  matrix products: 55.2 us -> 20.6 us
  local copies, waits for them, and re-layouts: 39.9 us -> 31.3 us
    pallas_call x0 -> x1, Pallas kernels: none -> 241 us  [keys_and_values(): pl.pallas_call(functools.partial(project_kernel, n_seq, n_head), out_shap...]
    all_gather x3 -> x1, waiting for transfers between devices: 190 us -> 11.1 us  [gather_halves(): mine = lax.all_gather(column_half(weight), 'seq', axis=0, tiled=True)]
    all_gather x2 -> x1, waiting for transfers between devices: 100 us -> 48.7 us  [partial_query(): rows = lax.all_gather(turned, 'head', axis=0, tiled=True)]
    dot_general x6 -> x2, matrix products: 42.2 us -> 7.69 us  [project(): jnp.dot(rows, half, preferred_element_type=jnp.float32)]
    ppermute x3 -> x1, waiting for transfers between devices: 35 us -> 20.3 us  [gather_halves(): other = lax.ppermute(mine, 'groups', [(0, 1), (1, 0)])]
    dynamic_slice x3 -> x1, local copies, waits for them, and re-layouts: 6.85 us -> 1.09 us  [column_half(): lax.dynamic_slice_in_dim(weight, lax.axis_index('groups') * cols, cols, a...]
  transfers between devices with their start and end apart: 12 -> 7, of which waited for: 10 -> 5; matrix products, arithmetic and copies ran while one was open for 18% -> 10% of each run, Pallas kernels for 0% -> 47%
where the time goes in v3:
time: 510 us
  Pallas kernels  241 us (47%)
  waiting for transfers between devices  147 us (29%)
  blocking collectives  40.6 us (8%)
  local copies, waits for them, and re-layouts  31.3 us (6%)
  matrix products  20.6 us (4%)
  other arithmetic  13.7 us (3%)
  between operations  13.4 us (3%)
    pallas_call x1, Pallas kernels, keys_and_values(): pl.pallas_call(functools.partial(project_kernel, n_seq, n_head), out_shap...  241 us
    all_gather x1, waiting for transfers between devices, partial_query(): rows = lax.all_gather(turned, 'head', axis=0, tiled=True)  48.7 us
    reduce_scatter x1, waiting for transfers between devices, local(): context = lax.psum_scatter(context, 'seq', scatter_dimension=0, tiled=True)  43.3 us
    all_gather x1, waiting for transfers between devices, local(): lax.all_gather(context, 'head', axis=1, tiled=True)  23.3 us
    all_gather x1, blocking collectives, local(): tops, sums = lax.all_gather(jnp.stack([top, summed]), 'seq', axis=1)  20.4 us
    ppermute x1, waiting for transfers between devices, gather_halves(): other = lax.ppermute(mine, 'groups', [(0, 1), (1, 0)])  20.3 us
    all_gather x1, blocking collectives, local(): lax.all_gather(jnp.concatenate([nbr_shard, nbr_row], axis=1), 'seq', axis...  11.9 us
    all_gather x1, waiting for transfers between devices, gather_halves(): mine = lax.all_gather(column_half(weight), 'seq', axis=0, tiled=True)  11.1 us
  transfers between devices with their start and end apart: 7, of which 5 were waited for; matrix products, arithmetic and copies ran while one was open for 10% of the time, Pallas kernels for 47%

profile of v3, /device:TPU:0, one launch (start us, length us, event | category | flops | bytes accessed | tf_op | source)
XLA Modules:
  0.0 509.7 jit_solution(543001992420431345)
XLA Ops:
  6.5 1.4 fusion.5
  7.9 8.3 %psum.14 = f32[256,1]{0,1:T(1,128)S(1)} all-reduce(f32[256,1]{0,1:T(1,128)S(1)} %bitcast.48), channel_id=1, replica_groups=mesh['groups'=2,'seq'=4,'head'=4] {'head'}, use_global_device_ids=true, to_apply=%region_1.0 | all-reduce | flops 256 | bytes 2048 | tf_op jit(solution)/shard_map/psum | solution.py:33
  16.3 0.7 dynamic_slice.6
  17.0 1.2 fusion.7
  18.2 0.7 collective-permute-start
  18.9 0.8 copy-done.5
  19.8 48.7 %all-gather.6.cloned.1.call-done = bf16[1024,1024]{1,0:T(8,128)(2,1)} async-done(((bf16[256,1024]{1,0:T(8,128)(2,1)}), bf16[1024,1024]{1,0:T(8,128)(2,1)}) %all-gather.6.cloned.1.call-update) | async-done | bytes 2097168 | tf_op jit(solution)/shard_map/all_gather | solution.py:45
  68.5 3.9 multiply_convert_fusion
  73.0 1.9 copy.30
  75.1 240.9 %shard_map.91 = (bf16[1024,1024]{1,0:T(8,128)(2,1)}, bf16[1024,1024]{1,0:T(8,128)(2,1)}) custom-call(bf16[1024,1024]{1,0:T(8,128)(2,1)} %bitcast.49, bf16[1024,1024]{1,0:T(8,128)(2,1)} %w_key, bf16[1024,1024]{1,0:T(8,128)(2,1)} %w_value), custom_call_target="tpu_custom_call" | custom-call | flops 17179869184 | bytes 524288000 | tf_op jit(solution)/shard_map/pallas_call | solution.py:245
  316.0 1.1 constant_dynamic-slice_fusion
  317.3 11.9 %all-gather.1 = s32[4,4,4]{2,1,0:T(4,128)S(1)} all-gather(s32[1,4,4]{2,1,0:T(4,128)S(1)} %bitcast.46), channel_id=1, replica_groups=mesh['groups'=2,'seq'=4,'head'=4] {'seq'}, dimensions={0}, use_global_device_ids=true | all-gather | bytes 320 | tf_op jit(solution)/shard_map/all_gather | solution.py:283
  329.5 4.5 gather_fusion.1
  334.0 2.8 gather_fusion
  336.8 7.6 %broadcast_select_fusion = (bf16[16,128,1024]{2,1,0:T(8,128)(2,1)}, bf16[16,128,1024]{2,1,0:T(8,128)(2,1)}) fusion(bf16[16,128,1024]{2,1,0:T(8,128)(2,1)} %gather_fusion.1, pred[16]{0:T(512)(128)(4,1)S(1)} %compare_and_fusion, bf16[16,128,1024]{2,1,0:T(8,128)(2,1)} %gather_fusion), kind=kLoop, calls=%fused_computation.5 | loop fusion | flops 4194304 | bytes 16777232 | tf_op jit(solution)/shard_map/jit(_take)/select_n | solution.py:294
  344.4 6.4 %copy.29 = bf16[16,128,1024]{1,2,0:T(8,128)(2,1)} copy(bf16[16,128,1024]{2,1,0:T(8,128)(2,1)} %get-tuple-element.29) | data formatting | bytes 8388608 | tf_op jit(solution)/shard_map/jit(_take)/select_n | solution.py:295
  350.8 6.4 %copy.31 = bf16[16,128,1024]{1,2,0:T(8,128)(2,1)} copy(bf16[16,128,1024]{2,1,0:T(8,128)(2,1)} %get-tuple-element.28) | data formatting | bytes 8388608 | tf_op jit(solution)/shard_map/jit(_take)/select_n | solution.py:294
  357.2 4.1 select_reduce_fusion
  361.4 1.9 copy-done.2
  363.3 2.4 exponential_reduce_fusion
  365.7 20.4 %all-gather = f32[2,64,8,64]{3,2,1,0:T(8,128)S(1)} all-gather(f32[2,16,8,64]{3,2,1,0:T(8,128)S(1)} %pad_maximum_fusion.1), channel_id=2, replica_groups=mesh['groups'=2,'seq'=4,'head'=4] {'seq'}, dimensions={1}, use_global_device_ids=true | all-gather | bytes 327680 | tf_op jit(solution)/shard_map/all_gather | solution.py:301
  386.3 4.9 convert_bitcast_fusion
  391.2 1.8 copy.34
  392.9 2.0 copy.43
  395.0 11.1 %all-gather.10.cloned.1.call-done = bf16[4096,512]{1,0:T(8,128)(2,1)} async-done(((bf16[1024,512]{1,0:T(8,128)(2,1)}), bf16[4096,512]{1,0:T(8,128)(2,1)}) %all-gather.10.cloned.1.call-update) | async-done | bytes 4194320 | tf_op jit(solution)/shard_map/all_gather | solution.py:19
  406.2 1.5 collective-permute-start.1
  407.6 43.3 %reduce-scatter.2.cloned.1.call-done = bf16[256,1024]{1,0:T(8,128)(2,1)} async-done(((bf16[1024,1024]{1,0:T(8,128)(2,1)}), bf16[256,1024]{1,0:T(8,128)(2,1)}) %reduce-scatter.2.cloned.1.call-update) | async-done | bytes 524304 | tf_op jit(solution)/shard_map/reduce_scatter | solution.py:307
  450.9 23.3 %all-gather.8.cloned.1.call-done = bf16[256,4096]{1,0:T(8,128)(2,1)} async-done(((bf16[256,1024]{1,0:T(8,128)(2,1)}), bf16[256,4096]{1,0:T(8,128)(2,1)}) %all-gather.8.cloned.1.call-update) | async-done | bytes 2097168 | tf_op jit(solution)/shard_map/all_gather | solution.py:308
  474.3 4.2 fusion.12
  478.5 20.3 %collective-permute-done.1 = bf16[4096,512]{1,0:T(8,128)(2,1)} collective-permute-done((bf16[4096,512]{1,0:T(8,128)(2,1)}, bf16[4096,512]{1,0:T(8,128)(2,1)}, u32[]{:S(2)}, u32[]{:S(2)}) %collective-permute-start.1) | collective-permute-done | bytes 4194336 | tf_op jit(solution)/shard_map/ppermute | solution.py:20
  498.8 3.5 select_convert_fusion.1
  502.3 0.9 pad_maximum_fusion
  (45 shorter events, 1.5 us)
Async XLA Ops:
  6.5 62.0 %copy-start = (bf16[1024,1024]{1,0:T(8,128)(2,1)S(1)}, bf16[1024,1024]{1,0:T(8,128)(2,1)}, u32[]{:S(2)}) copy-start(bf16[1024,1024]{1,0:T(8,128)(2,1)} %param.13) | copy-start | bytes 6291460
  6.5 61.9 %all-gather.6.cloned.1.call-start = ((), (), s32[]{:S(2)}) async-start(), calls=%async_computation.1 | async-start | bytes 2621440 | tf_op jit(solution)/shard_map/all_gather | solution.py:45
  18.2 0.7 collective-permute-start
  18.9 0.8 copy-start.5
  19.7 337.5 %all-reduce.2.cloned.1.call-start = ((), (), s32[]{:S(2)}) async-start(), calls=%async_computation.2 | async-start | bytes 4194304 | tf_op jit(solution)/shard_map/psum | solution.py:59
  75.0 331.2 %all-gather.10.cloned.1.call-start = ((), (), s32[]{:S(2)}) async-start(), calls=%async_computation.5 | async-start | bytes 5242880 | tf_op jit(solution)/shard_map/all_gather | solution.py:19
  75.0 241.0 %copy-start.4 = (bf16[1024,1024]{1,0:T(8,128)(2,1)S(1)}, bf16[1024,1024]{1,0:T(8,128)(2,1)}, u32[]{:S(2)}) copy-start(bf16[1024,1024]{1,0:T(8,128)(2,1)} %param.16) | copy-start | bytes 6291460
  75.0 242.1 %copy-start.6 = (s32[4,2]{0,1:T(2,128)S(1)}, s32[4,2]{0,1:T(2,128)}, u32[]{:S(2)}) copy-start(s32[4,2]{0,1:T(2,128)} %param.19) | copy-start | bytes 100
  75.1 242.1 %copy-start.7 = (s32[4,2]{0,1:T(2,128)S(1)}, s32[4,2]{0,1:T(2,128)}, u32[]{:S(2)}) copy-start(s32[4,2]{0,1:T(2,128)} %param.18) | copy-start | bytes 100
  317.1 133.8 %reduce-scatter.2.cloned.1.call-start = ((), (), s32[]{:S(2)}) async-start(), calls=%async_computation.3 | async-start | bytes 2621440 | tf_op jit(solution)/shard_map/reduce_scatter | solution.py:307
  329.5 4.5 copy-start.3
  361.4 2.0 copy-start.2
  395.0 79.3 %all-gather.8.cloned.1.call-start = ((), (), s32[]{:S(2)}) async-start(), calls=%async_computation.4 | async-start | bytes 2621440 | tf_op jit(solution)/shard_map/all_gather | solution.py:308
  406.2 92.6 %collective-permute-start.1 = (bf16[4096,512]{1,0:T(8,128)(2,1)}, bf16[4096,512]{1,0:T(8,128)(2,1)}, u32[]{:S(2)}, u32[]{:S(2)}) collective-permute-start(bf16[4096,512]{1,0:T(8,128)(2,1)} %all-gather.10.cloned.1.call-done), channel_id=1, source_target_pairs={{0,16},{16,0},{1,17},{17,1},{2,18},{18,2},{3,19},{19,3},{4,20},{20... | collective-permute-start | bytes 12582920 | tf_op jit(solution)/shard_map/ppermute | solution.py:20
  474.3 24.6 %copy-start.8 = (bf16[256,4096]{1,0:T(8,128)(2,1)S(1)}, bf16[256,4096]{1,0:T(8,128)(2,1)}, u32[]{:S(2)}) copy-start(bf16[256,4096]{1,0:T(8,128)(2,1)} %all-gather.8.cloned.1.call-done) | copy-start | bytes 6291460
  474.3 28.9 %copy-start.1 = (bf16[1024,1024]{1,0:T(8,128)(2,1)S(1)}, bf16[1024,1024]{1,0:T(8,128)(2,1)}, u32[]{:S(2)}) copy-start(bf16[1024,1024]{1,0:T(8,128)(2,1)} %param.13) | copy-start | bytes 6291460
Sparse Core Ops, SparseCore 0:
  19.8 48.5 all-gather.5
  75.1 136.9 all-reduce.1
  317.2 88.8 all-gather.9
  408.4 42.4 reduce-scatter.1
  452.3 21.8 all-gather.7

commit v4 on v3

--- a/solution.py
+++ b/solution.py
@@ -10,15 +10,12 @@
 HD = 128
 
 
-def column_half(weight):
-    cols = weight.shape[1] // 2
-    return lax.dynamic_slice_in_dim(weight, lax.axis_index("groups") * cols, cols, axis=1)
-
-
-def gather_halves(weight):
-    mine = lax.all_gather(column_half(weight), "seq", axis=0, tiled=True)
-    other = lax.ppermute(mine, "groups", [(0, 1), (1, 0)])
-    return mine, other
+def shifted(pieces, axis):
+    num, me = lax.axis_size(axis), lax.axis_index(axis)
+    got = [pieces(0)]
+    for k in range(1, num):
+        got.append(lax.ppermute(pieces(k), axis, [(i, (i + k) % num) for i in range(num)]))
+    return got, lax.rem(me - jnp.arange(num) + num, num)
 
 
 def project(rows, halves):
@@ -42,21 +39,23 @@
     if num == lax.axis_size("head"):
         swap = [(a * num + b, b * num + a) for a in range(num) for b in range(num)]
         turned = lax.ppermute(normed, ("seq", "head"), swap)
-        rows = lax.all_gather(turned, "head", axis=0, tiled=True)
+        got, order = shifted(lambda k: turned, "head")
+        rows = jnp.concatenate(got, axis=0)
         part = jnp.dot(rows, w_query, preferred_element_type=jnp.float32) / scale
-        return part.astype(jnp.bfloat16)
+        return part.astype(jnp.bfloat16), order
     rows = lax.all_gather(normed, "head", axis=1, tiled=True)
     query = jnp.dot(
         rows,
         lax.all_gather(w_query, "seq", axis=0, tiled=True),
         preferred_element_type=jnp.float32,
     )
-    return (query / scale).astype(jnp.bfloat16)
-
-
-def whole_query(part):
-    if lax.axis_size("seq") == lax.axis_size("head"):
-        return lax.psum(part, "seq")
+    return (query / scale).astype(jnp.bfloat16), None
+
+
+def whole_query(part, order):
+    if order is not None:
+        query = lax.psum(part, "seq").reshape(order.shape[0], -1, part.shape[1])
+        return jnp.take(query, order, axis=0).reshape(part.shape)
     return lax.all_gather(part, "seq", axis=0, tiled=True)
 
 
@@ -64,8 +63,8 @@
 
 
 def project_kernel(
-    n_seq, n_head, database, w_key, w_value, keys, values, whole, held, total,
-    near_send, near_recv, side_send, side_recv, row_send, row_recv, row_copy,
+    n_seq, n_head, database, w_key, w_value, w_out, keys, values, out_half, whole, held, total,
+    near_send, near_recv, side_send, side_recv, row_send, row_recv, row_copy, out_copy,
 ):
     g, z, h = lax.axis_index("groups"), lax.axis_index("seq"), lax.axis_index("head")
     weights = (w_key, w_value)
@@ -147,6 +146,10 @@
         row_move(h, lax.rem(h + step, n_head)).start()
     keep = pltpu.make_async_copy(database, whole.at[:, columns(h)], row_copy)
     keep.start()
+    out_cols = out_half.shape[1]
+    chosen = w_out.at[:, pl.ds(pl.multiple_of(g * out_cols, out_cols), out_cols)]
+    hand_on = pltpu.make_async_copy(chosen, out_half, out_copy)
+    hand_on.start()
 
     def valid(d, way):
         return z - d >= 0 if way == 0 else z + d < n_seq
@@ -209,8 +212,10 @@
     if n_seq > 1:
         multiply(n_seq - 1)
 
-    keys[...] = total[0].astype(keys.dtype)
-    values[...] = total[1].astype(values.dtype)
+    for i in range(width // HD):
+        keys[i] = total[0, :, i * HD : (i + 1) * HD].astype(keys.dtype)
+        values[i] = total[1, :, i * HD : (i + 1) * HD].astype(values.dtype)
+    hand_on.wait()
 
     for step in range(1, n_head):
         row_move(h, lax.rem(h + step, n_head)).wait_send()
@@ -237,16 +242,17 @@
                         along(w, owner, way).wait_send()
 
 
-def keys_and_values(database, w_key, w_value):
+def keys_and_values(database, w_key, w_value, w_out):
     n_seq, n_head = lax.axis_size("seq"), lax.axis_size("head")
     rows, feats = database.shape
     depth, width = w_key.shape
     vmem = pl.BlockSpec(memory_space=pltpu.VMEM)
     return pl.pallas_call(
         functools.partial(project_kernel, n_seq, n_head),
-        out_shape=[jax.ShapeDtypeStruct((rows, width), jnp.bfloat16)] * 2,
-        in_specs=[pl.BlockSpec(memory_space=pl.ANY), vmem, vmem],
-        out_specs=[vmem, vmem],
+        out_shape=[jax.ShapeDtypeStruct((width // HD, rows, HD), jnp.bfloat16)] * 2
+        + [jax.ShapeDtypeStruct((w_out.shape[0], w_out.shape[1] // 2), jnp.bfloat16)],
+        in_specs=[pl.BlockSpec(memory_space=pl.ANY), vmem, vmem, pl.BlockSpec(memory_space=pl.ANY)],
+        out_specs=[vmem, vmem, pl.BlockSpec(memory_space=pl.ANY)],
         scratch_shapes=[
             pltpu.VMEM((rows, feats * n_head), jnp.bfloat16),
             pltpu.VMEM((2, depth * n_seq, width), jnp.bfloat16),
@@ -258,6 +264,7 @@
             pltpu.SemaphoreType.DMA((n_head,)),
             pltpu.SemaphoreType.DMA((n_head,)),
             pltpu.SemaphoreType.DMA,
+            pltpu.SemaphoreType.DMA,
         ],
         compiler_params=pltpu.CompilerParams(
             collective_id=0, has_side_effects=True, vmem_limit_bytes=56 * 1024 * 1024
@@ -267,44 +274,58 @@
             bytes_accessed=500 * 1024 * 1024,
             transcendentals=0,
         ),
-    )(database, w_key, w_value)
+    )(database, w_key, w_value, w_out)
 
 
 def local(tokens, norm_gain, w_query, w_key, w_value, w_out, database, nbr_shard, nbr_row):
     rows_dev, ntok, feat_dev = database.shape
-    part = partial_query(normalize(tokens, norm_gain), w_query)
+    part, order = partial_query(normalize(tokens, norm_gain), w_query)
+    own = jnp.concatenate([nbr_shard, nbr_row], axis=1)
+    got, by_seq = shifted(lambda k: own, "seq")
+    near = jnp.take(jnp.stack(got), by_seq, axis=0).reshape(-1, 4)
     part, w_key, w_value = lax.optimization_barrier((part, w_key, w_value))
-    query = whole_query(part)
-    keys, values = keys_and_values(database.reshape(rows_dev * ntok, feat_dev), w_key, w_value)
-    keys, values, w_out = lax.optimization_barrier((keys, values, w_out))
-    out_halves = gather_halves(w_out)
-
-    me = lax.axis_index("seq")
-    near = lax.all_gather(jnp.concatenate([nbr_shard, nbr_row], axis=1), "seq", axis=0, tiled=True)
+    query = whole_query(part, order)
+    flat = database.reshape(rows_dev * ntok, feat_dev)
+    keys, values, out_half = keys_and_values(flat, w_key, w_value, w_out)
+    out_mine = lax.all_gather(out_half, "seq", axis=0, tiled=True)
+    out_halves = out_mine, lax.ppermute(out_mine, "groups", [(0, 1), (1, 0)])
+
+    num, me = lax.axis_size("seq"), lax.axis_index("seq")
     here = near[:, :2] == me
     mine = jnp.any(here, axis=1)
     row = jnp.sum(jnp.where(here, near[:, 2:], 0), axis=1)
-
     spans = near.shape[0]
+    spans_dev = spans // num
     width = w_key.shape[1]
     heads_dev = width // HD
     span_len = query.shape[0] // spans
-    keys = keys.reshape(rows_dev, ntok, width)
-    values = values.reshape(rows_dev, ntok, width)
-    keys = jnp.take(keys, row, axis=0).reshape(spans, ntok, heads_dev, HD)
-    values = jnp.take(values, row, axis=0).reshape(spans, ntok, heads_dev, HD)
-    qh = query.reshape(spans, span_len, heads_dev, HD)
-    scores = jnp.einsum("cqhd,ckhd->chqk", qh, keys, preferred_element_type=jnp.float32)
-    scores = jnp.where(mine[:, None, None, None], scores, -jnp.inf)
-    top = jnp.max(scores, axis=-1)
-    summed = jnp.sum(jnp.exp(scores - jnp.where(jnp.isfinite(top), top, 0.0)[..., None]), axis=-1)
-    tops, sums = lax.all_gather(jnp.stack([top, summed]), "seq", axis=1)
-    most = jnp.max(tops, axis=0)
-    denominator = jnp.sum(jnp.exp(tops - most) * sums, axis=0)
-    weights = (jnp.exp(scores - most[..., None]) / denominator[..., None]).astype(jnp.bfloat16)
-    context = jnp.einsum("chqk,ckhd->cqhd", weights, values, preferred_element_type=jnp.float32)
-    context = context.astype(jnp.bfloat16).reshape(spans * span_len, width)
-    context = lax.psum_scatter(context, "seq", scatter_dimension=0, tiled=True)
+    keys = jnp.take(keys.reshape(heads_dev, rows_dev, ntok, HD), row, axis=1)
+    values = jnp.take(values.reshape(heads_dev, rows_dev, ntok, HD), row, axis=1)
+    qh = query.reshape(spans, span_len, heads_dev, HD).transpose(2, 0, 1, 3)
+    scores = jnp.einsum("hcqd,hckd->hcqk", qh, keys, preferred_element_type=jnp.float32)
+    top = jnp.max(scores, axis=-1, keepdims=True)
+    raised = jnp.exp(scores - top)
+    summed = jnp.sum(raised, axis=-1, keepdims=True)
+    weights = (raised / summed).astype(jnp.bfloat16)
+    context = jnp.einsum("hcqk,hckd->hcqd", weights, values, preferred_element_type=jnp.float32)
+    context = context.astype(jnp.bfloat16)
+    top = jnp.where(mine[:, None], top[..., 0], -jnp.inf)
+    stats = jnp.stack([top, summed[..., 0]])
+
+    def for_device(array, axis):
+        def piece(k):
+            start = lax.rem(me + k, num) * spans_dev
+            return lax.dynamic_slice_in_dim(array, start, spans_dev, axis=axis)
+
+        return piece
+
+    stats = jnp.stack(shifted(for_device(stats, 2), "seq")[0])
+    tops, sums = stats[:, 0], stats[:, 1]
+    shares = jnp.exp(tops - jnp.max(tops, axis=0)) * sums
+    shares = shares / jnp.sum(shares, axis=0)
+    pieces = shifted(for_device(context, 1), "seq")[0]
+    context = sum(shares[i][..., None] * piece.astype(jnp.float32) for i, piece in enumerate(pieces))
+    context = context.astype(jnp.bfloat16).transpose(1, 2, 0, 3).reshape(spans_dev * span_len, width)
     attended = project(lax.all_gather(context, "head", axis=1, tiled=True), out_halves)
     return attended.astype(jnp.bfloat16)
 

time: 510 us -> 547 us (1.073)
  waiting for transfers between devices: 147 us -> 198 us
  starting transfers between devices: 2.34 us -> 41.2 us
  blocking collectives: 40.6 us -> 8.34 us
  local copies, waits for them, and re-layouts: 31.3 us -> 16.3 us
  Pallas kernels: 241 us -> 235 us
    ppermute x1 -> x13, waiting for transfers between devices: 20.3 us -> 91.5 us  [the longest x1 63.8 us: local(): out_halves = (out_mine, lax.ppermute(out_mine, 'groups', [(0, 1), (1, 0)]))]
    reduce_scatter x1 -> x0, waiting for transfers between devices: 43.3 us -> none  [local(): context = lax.psum_scatter(context, 'seq', scatter_dimension=0, tiled=True)]
    ppermute x1 -> x13, starting transfers between devices: 1.47 us -> 40.4 us  [the longest x12 38.9 us: shifted(): lax.ppermute(pieces(k), axis, [(i, (i + k) % num) for i in range(num)])]
    all_gather x2 -> x0, blocking collectives: 32.3 us -> none  [the longest x1 20.4 us: local(): tops, sums = lax.all_gather(jnp.stack([top, summed]), 'seq', axis=1)]
    all_gather x2 -> x1, waiting for transfers between devices: 59.9 us -> 87.4 us  [local(): out_mine = lax.all_gather(out_half, 'seq', axis=0, tiled=True)]
    select_n x2 -> x0, local copies, waits for them, and re-layouts: 12.8 us -> none  [the longest x1 6.43 us: local(): values = jnp.take(values, row, axis=0).reshape(spans, ntok, heads_dev, HD)]
    pallas_call x1, Pallas kernels: 241 us -> 235 us  [keys_and_values(): pl.pallas_call(functools.partial(project_kernel, n_seq, n_head), out_shap...]
  transfers between devices with their start and end apart: 7 -> 17, of which waited for: 5 -> 7; matrix products, arithmetic and copies ran while one was open for 10% -> 7% of each run, Pallas kernels for 47% -> 43%
where the time goes in v4:
time: 547 us
  Pallas kernels  235 us (43%)
  waiting for transfers between devices  198 us (36%)
  starting transfers between devices  41.2 us (8%)
  matrix products  17.3 us (3%)
  other arithmetic  16.5 us (3%)
  local copies, waits for them, and re-layouts  16.3 us (3%)
  between operations  13.4 us (2%)
  blocking collectives  8.34 us (2%)
    pallas_call x1, Pallas kernels, keys_and_values(): pl.pallas_call(functools.partial(project_kernel, n_seq, n_head), out_shap...  235 us
    all_gather x1, waiting for transfers between devices, local(): out_mine = lax.all_gather(out_half, 'seq', axis=0, tiled=True)  87.4 us
    ppermute x1, waiting for transfers between devices, local(): out_halves = (out_mine, lax.ppermute(out_mine, 'groups', [(0, 1), (1, 0)]))  63.8 us
    ppermute x12, starting transfers between devices, shifted(): lax.ppermute(pieces(k), axis, [(i, (i + k) % num) for i in range(num)])  38.9 us
    ppermute x12, waiting for transfers between devices, shifted(): lax.ppermute(pieces(k), axis, [(i, (i + k) % num) for i in range(num)])  27.7 us
    all_gather x1, waiting for transfers between devices, local(): lax.all_gather(context, 'head', axis=1, tiled=True)  19.1 us
  transfers between devices with their start and end apart: 17, of which 7 were waited for; matrix products, arithmetic and copies ran while one was open for 7% of the time, Pallas kernels for 43%

profile of v4, /device:TPU:0, one launch (start us, length us, event | category | flops | bytes accessed | tf_op | source)
XLA Modules:
  0.0 546.6 jit_solution(15865276762492491934)
XLA Ops:
  6.5 1.4 fusion.19
  7.9 8.3 %psum.14 = f32[256,1]{0,1:T(1,128)S(1)} all-reduce(f32[256,1]{0,1:T(1,128)S(1)} %bitcast.95), channel_id=1, replica_groups=mesh['groups'=2,'seq'=4,'head'=4] {'head'}, use_global_device_ids=true, to_apply=%region_2.3 | all-reduce | flops 256 | bytes 2048 | tf_op jit(solution)/shard_map/psum | solution.py:30
  17.0 1.2 fusion.21
  18.9 17.5 %collective-permute-start.6 = (bf16[256,1024]{1,0:T(8,128)(2,1)S(1)}, bf16[256,1024]{1,0:T(8,128)(2,1)S(1)}, u32[]{:S(2)}, u32[]{:S(2)}) collective-permute-start(bf16[256,1024]{1,0:T(8,128)(2,1)S(1)} %collective-permute-done.3), channel_id=1, source_target_pairs={{0,3},{1,0},{2,1},{3,2},{4,7},{5,4},{6,5},{7,6},{8,11},{9,8},{10,9... | collective-permute-start | bytes 1572872 | tf_op jit(solution)/shard_map/ppermute | solution.py:17
  36.4 11.7 %collective-permute-start.5 = (bf16[256,1024]{1,0:T(8,128)(2,1)S(1)}, bf16[256,1024]{1,0:T(8,128)(2,1)S(1)}, u32[]{:S(2)}, u32[]{:S(2)}) collective-permute-start(bf16[256,1024]{1,0:T(8,128)(2,1)S(1)} %collective-permute-done.3), channel_id=1, source_target_pairs={{0,2},{1,3},{2,0},{3,1},{4,6},{5,7},{6,4},{7,5},{8,10},{9,11},{10,... | collective-permute-start | bytes 1572872 | tf_op jit(solution)/shard_map/ppermute | solution.py:17
  48.3 23.6 %collective-permute-done.5 = bf16[256,1024]{1,0:T(8,128)(2,1)S(1)} collective-permute-done((bf16[256,1024]{1,0:T(8,128)(2,1)S(1)}, bf16[256,1024]{1,0:T(8,128)(2,1)S(1)}, u32[]{:S(2)}, u32[]{:S(2)}) %collective-permute-start.5) | collective-permute-done | bytes 524320 | tf_op jit(solution)/shard_map/ppermute | solution.py:17
  71.9 3.6 multiply_convert_fusion
  75.6 235.4 %shard_map.91 = (bf16[8,1024,128]{2,1,0:T(8,128)(2,1)}, bf16[8,1024,128]{2,1,0:T(8,128)(2,1)}, bf16[1024,512]{1,0:T(8,128)(2,1)}) custom-call(bf16[1024,1024]{1,0:T(8,128)(2,1)} %bitcast.96, bf16[1024,1024]{1,0:T(8,128)(2,1)} %w_key, bf16[1024,1024]{1,0:T(8,128)(2,1)} %w_value, bf16[1024,1024]{1,0:T(8,128)(2,1)} %w_out.1), custom_call_target="tpu_custom_call" | custom-call | flops 17179869184 | bytes 524288000 | tf_op jit(solution)/shard_map/pallas_call | solution.py:250
  311.2 1.8 collective-permute-start.2
  314.9 2.6 collective-permute-done.1
  319.2 4.8 gather_fusion.2
  324.0 3.0 gather_fusion.3
  327.1 7.5 %select_bitcast_fusion.1 = (bf16[8,16,128,128]{3,2,0,1:T(8,128)(2,1)}, bf16[8,16,128,128]{3,2,0,1:T(8,128)(2,1)}) fusion(bf16[16,8,128,128]{3,2,1,0:T(8,128)(2,1)} %gather_fusion.2, pred[16]{0:T(512)(128)(4,1)S(1)} %compare_and_fusion, bf16[16,8,128,128]{3,2,1,0:T(8,128)(2,1)} %gather_fusion.3), kind=kLoop, calls=%fused_computation.9 | loop fusion | flops 4194304 | bytes 16777232 | tf_op jit(solution)/shard_map/jit(_take)/select_n | solution.py:302
  334.6 2.3 gather_fusion.1
  337.8 1.3 copy-done.2
  339.1 3.1 fusion.39
  342.2 2.4 fusion.4
  344.7 1.1 collective-permute-start.9
  346.0 1.9 collective-permute-start.7
  347.9 3.0 fusion.16
  350.9 1.0 constant_dynamic-slice_fusion.2
  351.9 1.9 collective-permute-start.12
  353.8 1.0 collective-permute-start.11
  354.8 0.9 collective-permute-start.10
  355.8 87.4 %all-gather.5.cloned.1.call-done = bf16[4096,512]{1,0:T(8,128)(2,1)} async-done(((bf16[1024,512]{1,0:T(8,128)(2,1)}), bf16[4096,512]{1,0:T(8,128)(2,1)}) %all-gather.5.cloned.1.call-update) | async-done | bytes 4194320 | tf_op jit(solution)/shard_map/all_gather | solution.py:290
  443.3 1.5 collective-permute-start.13
  444.9 2.4 fusion.22
  447.7 0.9 copy.43
  448.6 19.1 %all-gather.3.cloned.1.call-done = bf16[256,4096]{1,0:T(8,128)(2,1)} async-done(((bf16[256,1024]{1,0:T(8,128)(2,1)}), bf16[256,4096]{1,0:T(8,128)(2,1)}) %all-gather.3.cloned.1.call-update) | async-done | bytes 2097168 | tf_op jit(solution)/shard_map/all_gather | solution.py:329
  467.7 4.2 fusion.40
  471.9 63.8 %collective-permute-done.13 = bf16[4096,512]{1,0:T(8,128)(2,1)} collective-permute-done((bf16[4096,512]{1,0:T(8,128)(2,1)}, bf16[4096,512]{1,0:T(8,128)(2,1)}, u32[]{:S(2)}, u32[]{:S(2)}) %collective-permute-start.13) | collective-permute-done | bytes 4194336 | tf_op jit(solution)/shard_map/ppermute | solution.py:291
  535.7 3.5 select_convert_fusion.1
  (74 shorter events, 7.9 us)
Async XLA Ops:
  6.5 65.4 %copy-start = (bf16[1024,1024]{1,0:T(8,128)(2,1)S(1)}, bf16[1024,1024]{1,0:T(8,128)(2,1)}, u32[]{:S(2)}) copy-start(bf16[1024,1024]{1,0:T(8,128)(2,1)} %param.13) | copy-start | bytes 6291460
  6.5 328.1 %all-reduce.2.cloned.1.call-start = ((), (), s32[]{:S(2)}) async-start(), calls=%async_computation | async-start | bytes 4194304 | tf_op jit(solution)/shard_map/psum | solution.py:57
  18.2 0.7 collective-permute-start.3
  18.9 29.4 %collective-permute-start.6 = (bf16[256,1024]{1,0:T(8,128)(2,1)S(1)}, bf16[256,1024]{1,0:T(8,128)(2,1)S(1)}, u32[]{:S(2)}, u32[]{:S(2)}) collective-permute-start(bf16[256,1024]{1,0:T(8,128)(2,1)S(1)} %collective-permute-done.3), channel_id=1, source_target_pairs={{0,3},{1,0},{2,1},{3,2},{4,7},{5,4},{6,5},{7,6},{8,11},{9,8},{10,9... | collective-permute-start | bytes 1572872 | tf_op jit(solution)/shard_map/ppermute | solution.py:17
  36.4 35.5 %collective-permute-start.5 = (bf16[256,1024]{1,0:T(8,128)(2,1)S(1)}, bf16[256,1024]{1,0:T(8,128)(2,1)S(1)}, u32[]{:S(2)}, u32[]{:S(2)}) collective-permute-start(bf16[256,1024]{1,0:T(8,128)(2,1)S(1)} %collective-permute-done.3), channel_id=1, source_target_pairs={{0,2},{1,3},{2,0},{3,1},{4,6},{5,7},{6,4},{7,5},{8,10},{9,11},{10,... | collective-permute-start | bytes 1572872 | tf_op jit(solution)/shard_map/ppermute | solution.py:17
  48.1 23.8 %collective-permute-start.4 = (bf16[256,1024]{1,0:T(8,128)(2,1)S(1)}, bf16[256,1024]{1,0:T(8,128)(2,1)S(1)}, u32[]{:S(2)}, u32[]{:S(2)}) collective-permute-start(bf16[256,1024]{1,0:T(8,128)(2,1)S(1)} %collective-permute-done.3), channel_id=1, source_target_pairs={{0,1},{1,2},{2,3},{3,0},{4,5},{5,6},{6,7},{7,4},{8,9},{9,10},{10,1... | collective-permute-start | bytes 1572872 | tf_op jit(solution)/shard_map/ppermute | solution.py:17
  75.5 367.7 %all-gather.5.cloned.1.call-start = ((), (), s32[]{:S(2)}) async-start(), calls=%async_computation.2 | async-start | bytes 5242880 | tf_op jit(solution)/shard_map/all_gather | solution.py:290
  75.6 235.5 %copy-start.5 = (s32[4,2]{0,1:T(2,128)S(1)}, s32[4,2]{0,1:T(2,128)}, u32[]{:S(2)}) copy-start(s32[4,2]{0,1:T(2,128)} %param.19) | copy-start | bytes 100
  75.6 235.5 %copy-start.6 = (s32[4,2]{0,1:T(2,128)S(1)}, s32[4,2]{0,1:T(2,128)}, u32[]{:S(2)}) copy-start(s32[4,2]{0,1:T(2,128)} %param.18) | copy-start | bytes 100
  311.1 156.6 %all-gather.3.cloned.1.call-start = ((), (), s32[]{:S(2)}) async-start(), calls=%async_computation.1 | async-start | bytes 2621440 | tf_op jit(solution)/shard_map/all_gather | solution.py:329
  311.2 3.6 collective-permute-start.2
  313.0 4.5 collective-permute-start.1
  313.0 5.4 collective-permute-start
  319.2 4.8 copy-start.3
  336.9 2.2 copy-start.2
  342.2 5.8 %copy-start.4 = (bf16[8,16,128,128]{3,2,0,1:T(8,128)(2,1)S(1)}, bf16[8,16,128,128]{3,2,0,1:T(8,128)(2,1)}, u32[]{:S(2)}) copy-start(bf16[8,16,128,128]{3,2,0,1:T(8,128)(2,1)} %get-tuple-element.32) | copy-start | bytes 12582916
  344.7 10.1 %collective-permute-start.9 = (f32[2,8,4,64]{3,2,1,0:T(4,128)S(1)}, f32[2,8,4,64]{3,2,1,0:T(4,128)S(1)}, u32[]{:S(2)}, u32[]{:S(2)}) collective-permute-start(f32[2,8,4,64]{3,2,1,0:T(4,128)S(1)} %get-tuple-element.26), channel_id=1, source_target_pairs={{0,12},{4,0},{8,4},{12,8},{1,13},{5,1},{9,5},{13,9},{2,14},{6,2},{... | collective-permute-start | bytes 49160 | tf_op jit(solution)/shard_map/ppermute | solution.py:17
  345.9 9.8 %collective-permute-start.8 = (f32[2,8,4,64]{3,2,1,0:T(4,128)S(1)}, f32[2,8,4,64]{3,2,1,0:T(4,128)S(1)}, u32[]{:S(2)}, u32[]{:S(2)}) collective-permute-start(f32[2,8,4,64]{3,2,1,0:T(4,128)S(1)} %get-tuple-element.25), channel_id=1, source_target_pairs={{0,8},{4,12},{8,0},{12,4},{1,9},{5,13},{9,1},{13,5},{2,10},{6,14},... | collective-permute-start | bytes 49160 | tf_op jit(solution)/shard_map/ppermute | solution.py:17
  346.0 9.7 %collective-permute-start.7 = (f32[2,8,4,64]{3,2,1,0:T(4,128)S(1)}, f32[2,8,4,64]{3,2,1,0:T(4,128)S(1)}, u32[]{:S(2)}, u32[]{:S(2)}) collective-permute-start(f32[2,8,4,64]{3,2,1,0:T(4,128)S(1)} %get-tuple-element.24), channel_id=1, source_target_pairs={{0,4},{4,8},{8,12},{12,0},{1,5},{5,9},{9,13},{13,1},{2,6},{6,10},{... | collective-permute-start | bytes 49160 | tf_op jit(solution)/shard_map/ppermute | solution.py:17
  351.9 93.0 %collective-permute-start.12 = (bf16[8,4,64,128]{3,2,1,0:T(8,128)(2,1)}, bf16[8,4,64,128]{3,2,1,0:T(8,128)(2,1)}, u32[]{:S(2)}, u32[]{:S(2)}) collective-permute-start(bf16[8,4,64,128]{3,2,1,0:T(8,128)(2,1)} %get-tuple-element.19), channel_id=1, source_target_pairs={{0,12},{4,0},{8,4},{12,8},{1,13},{5,1},{9,5},{13,9},{2,14},{6,2},{... | collective-permute-start | bytes 1572872 | tf_op jit(solution)/shard_map/ppermute | solution.py:17
  353.8 91.1 %collective-permute-start.11 = (bf16[8,4,64,128]{3,2,1,0:T(8,128)(2,1)S(1)}, bf16[8,4,64,128]{3,2,1,0:T(8,128)(2,1)}, u32[]{:S(2)}, u32[]{:S(2)}) collective-permute-start(bf16[8,4,64,128]{3,2,1,0:T(8,128)(2,1)S(1)} %get-tuple-element.20), channel_id=1, source_target_pairs={{0,8},{4,12},{8,0},{12,4},{1,9},{5,13},{9,1},{13,5},{2,10},{6,14},... | collective-permute-start | bytes 1572872 | tf_op jit(solution)/shard_map/ppermute | solution.py:17
  354.8 90.1 %collective-permute-start.10 = (bf16[8,4,64,128]{3,2,1,0:T(8,128)(2,1)S(1)}, bf16[8,4,64,128]{3,2,1,0:T(8,128)(2,1)}, u32[]{:S(2)}, u32[]{:S(2)}) collective-permute-start(bf16[8,4,64,128]{3,2,1,0:T(8,128)(2,1)S(1)} %get-tuple-element.18), channel_id=1, source_target_pairs={{0,4},{4,8},{8,12},{12,0},{1,5},{5,9},{9,13},{13,1},{2,6},{6,10},{... | collective-permute-start | bytes 1572872 | tf_op jit(solution)/shard_map/ppermute | solution.py:17
  443.3 92.4 %collective-permute-start.13 = (bf16[4096,512]{1,0:T(8,128)(2,1)}, bf16[4096,512]{1,0:T(8,128)(2,1)}, u32[]{:S(2)}, u32[]{:S(2)}) collective-permute-start(bf16[4096,512]{1,0:T(8,128)(2,1)} %all-gather.5.cloned.1.call-done), channel_id=1, source_target_pairs={{0,16},{16,0},{1,17},{17,1},{2,18},{18,2},{3,19},{19,3},{4,20},{20... | collective-permute-start | bytes 12582920 | tf_op jit(solution)/shard_map/ppermute | solution.py:291
  467.7 68.0 %copy-start.7 = (bf16[256,4096]{1,0:T(8,128)(2,1)S(1)}, bf16[256,4096]{1,0:T(8,128)(2,1)}, u32[]{:S(2)}) copy-start(bf16[256,4096]{1,0:T(8,128)(2,1)} %all-gather.3.cloned.1.call-done) | copy-start | bytes 6291460
  467.7 72.3 %copy-start.1 = (bf16[1024,1024]{1,0:T(8,128)(2,1)S(1)}, bf16[1024,1024]{1,0:T(8,128)(2,1)}, u32[]{:S(2)}) copy-start(bf16[1024,1024]{1,0:T(8,128)(2,1)} %param.13) | copy-start | bytes 6291460
Sparse Core Ops, SparseCore 0:
  75.7 135.4 all-reduce.1
  311.2 132.0 all-gather.4
  448.7 18.9 all-gather.2

commit v5 on v4

--- a/solution.py
+++ b/solution.py
@@ -16,12 +16,6 @@
     for k in range(1, num):
         got.append(lax.ppermute(pieces(k), axis, [(i, (i + k) % num) for i in range(num)]))
     return got, lax.rem(me - jnp.arange(num) + num, num)
-
-
-def project(rows, halves):
-    mine, other = (jnp.dot(rows, half, preferred_element_type=jnp.float32) for half in halves)
-    first = lax.axis_index("groups") == 0
-    return jnp.concatenate([jnp.where(first, mine, other), jnp.where(first, other, mine)], axis=1)
 
 
 def normalize(tokens, norm_gain):
@@ -63,8 +57,8 @@
 
 
 def project_kernel(
-    n_seq, n_head, database, w_key, w_value, w_out, keys, values, out_half, whole, held, total,
-    near_send, near_recv, side_send, side_recv, row_send, row_recv, row_copy, out_copy,
+    n_seq, n_head, database, w_key, w_value, keys, values, whole, held, total,
+    near_send, near_recv, side_send, side_recv, row_send, row_recv, row_copy,
 ):
     g, z, h = lax.axis_index("groups"), lax.axis_index("seq"), lax.axis_index("head")
     weights = (w_key, w_value)
@@ -146,10 +140,6 @@
         row_move(h, lax.rem(h + step, n_head)).start()
     keep = pltpu.make_async_copy(database, whole.at[:, columns(h)], row_copy)
     keep.start()
-    out_cols = out_half.shape[1]
-    chosen = w_out.at[:, pl.ds(pl.multiple_of(g * out_cols, out_cols), out_cols)]
-    hand_on = pltpu.make_async_copy(chosen, out_half, out_copy)
-    hand_on.start()
 
     def valid(d, way):
         return z - d >= 0 if way == 0 else z + d < n_seq
@@ -215,7 +205,6 @@
     for i in range(width // HD):
         keys[i] = total[0, :, i * HD : (i + 1) * HD].astype(keys.dtype)
         values[i] = total[1, :, i * HD : (i + 1) * HD].astype(values.dtype)
-    hand_on.wait()
 
     for step in range(1, n_head):
         row_move(h, lax.rem(h + step, n_head)).wait_send()
@@ -242,17 +231,16 @@
                         along(w, owner, way).wait_send()
 
 
-def keys_and_values(database, w_key, w_value, w_out):
+def keys_and_values(database, w_key, w_value):
     n_seq, n_head = lax.axis_size("seq"), lax.axis_size("head")
     rows, feats = database.shape
     depth, width = w_key.shape
     vmem = pl.BlockSpec(memory_space=pltpu.VMEM)
     return pl.pallas_call(
         functools.partial(project_kernel, n_seq, n_head),
-        out_shape=[jax.ShapeDtypeStruct((width // HD, rows, HD), jnp.bfloat16)] * 2
-        + [jax.ShapeDtypeStruct((w_out.shape[0], w_out.shape[1] // 2), jnp.bfloat16)],
-        in_specs=[pl.BlockSpec(memory_space=pl.ANY), vmem, vmem, pl.BlockSpec(memory_space=pl.ANY)],
-        out_specs=[vmem, vmem, pl.BlockSpec(memory_space=pl.ANY)],
+        out_shape=[jax.ShapeDtypeStruct((width // HD, rows, HD), jnp.bfloat16)] * 2,
+        in_specs=[pl.BlockSpec(memory_space=pl.ANY), vmem, vmem],
+        out_specs=[vmem, vmem],
         scratch_shapes=[
             pltpu.VMEM((rows, feats * n_head), jnp.bfloat16),
             pltpu.VMEM((2, depth * n_seq, width), jnp.bfloat16),
@@ -264,7 +252,6 @@
             pltpu.SemaphoreType.DMA((n_head,)),
             pltpu.SemaphoreType.DMA((n_head,)),
             pltpu.SemaphoreType.DMA,
-            pltpu.SemaphoreType.DMA,
         ],
         compiler_params=pltpu.CompilerParams(
             collective_id=0, has_side_effects=True, vmem_limit_bytes=56 * 1024 * 1024
@@ -274,7 +261,7 @@
             bytes_accessed=500 * 1024 * 1024,
             transcendentals=0,
         ),
-    )(database, w_key, w_value, w_out)
+    )(database, w_key, w_value)
 
 
 def local(tokens, norm_gain, w_query, w_key, w_value, w_out, database, nbr_shard, nbr_row):
@@ -286,9 +273,11 @@
     part, w_key, w_value = lax.optimization_barrier((part, w_key, w_value))
     query = whole_query(part, order)
     flat = database.reshape(rows_dev * ntok, feat_dev)
-    keys, values, out_half = keys_and_values(flat, w_key, w_value, w_out)
-    out_mine = lax.all_gather(out_half, "seq", axis=0, tiled=True)
-    out_halves = out_mine, lax.ppermute(out_mine, "groups", [(0, 1), (1, 0)])
+    keys, values = keys_and_values(flat, w_key, w_value)
+    cols = w_out.shape[1] // 2
+    part_of = lax.axis_index("groups")
+    chosen = lax.dynamic_slice_in_dim(w_out, part_of * cols, cols, axis=1)
+    out_mine = lax.all_gather(chosen, "seq", axis=0, tiled=True)
 
     num, me = lax.axis_size("seq"), lax.axis_index("seq")
     here = near[:, :2] == me
@@ -326,7 +315,20 @@
     pieces = shifted(for_device(context, 1), "seq")[0]
     context = sum(shares[i][..., None] * piece.astype(jnp.float32) for i, piece in enumerate(pieces))
     context = context.astype(jnp.bfloat16).transpose(1, 2, 0, 3).reshape(spans_dev * span_len, width)
-    attended = project(lax.all_gather(context, "head", axis=1, tiled=True), out_halves)
+    whole = lax.all_gather(context, "head", axis=1, tiled=True)
+    depth = w_out.shape[0]
+    left = lax.dynamic_slice_in_dim(w_out, (1 - part_of) * cols, cols, axis=1)
+    other = 0.0
+    for k in range(num):
+        start = lax.rem(me + k, num) * depth
+        if k > 0:
+            block = lax.dynamic_slice_in_dim(out_mine, start, depth, axis=0)
+            left = lax.ppermute(block, "groups", [(0, 1), (1, 0)])
+        rows = lax.dynamic_slice_in_dim(whole, start, depth, axis=1)
+        other = other + jnp.dot(rows, left, preferred_element_type=jnp.float32)
+    mine = jnp.dot(whole, out_mine, preferred_element_type=jnp.float32)
+    first = part_of == 0
+    attended = jnp.concatenate([jnp.where(first, mine, other), jnp.where(first, other, mine)], axis=1)
     return attended.astype(jnp.bfloat16)
 
 

time: 547 us -> 547 us (level)
  waiting for transfers between devices: 198 us -> 129 us
  Pallas kernels: 235 us -> 298 us
    all_gather x2, waiting for transfers between devices: 107 us -> 14.8 us  [the longest x1 14.8 us: local(): whole = lax.all_gather(context, 'head', axis=1, tiled=True)]
    pallas_call x1, Pallas kernels: 235 us -> 298 us  [keys_and_values(): pl.pallas_call(functools.partial(project_kernel, n_seq, n_head), out_shap...]
    ppermute x12, waiting for transfers between devices: 27.7 us -> 70.4 us  [shifted(): lax.ppermute(pieces(k), axis, [(i, (i + k) % num) for i in range(num)])]
    ppermute x1 -> x3, waiting for transfers between devices: 63.8 us -> 43.3 us  [local(): left = lax.ppermute(block, 'groups', [(0, 1), (1, 0)])]
  transfers between devices with their start and end apart: 17 -> 19, of which waited for: 7 -> 9; matrix products, arithmetic and copies ran while one was open for 7% -> 8% of each run, Pallas kernels for 43% -> 54%
where the time goes in v5:
time: 547 us
  Pallas kernels  298 us (54%)
  waiting for transfers between devices  129 us (24%)
  starting transfers between devices  42.6 us (8%)
  local copies, waits for them, and re-layouts  21.7 us (4%)
  matrix products  18.8 us (3%)
  other arithmetic  15.3 us (3%)
  between operations  13.5 us (2%)
  blocking collectives  8.34 us (2%)
    pallas_call x1, Pallas kernels, keys_and_values(): pl.pallas_call(functools.partial(project_kernel, n_seq, n_head), out_shap...  298 us
    ppermute x12, waiting for transfers between devices, shifted(): lax.ppermute(pieces(k), axis, [(i, (i + k) % num) for i in range(num)])  70.4 us
    ppermute x3, waiting for transfers between devices, local(): left = lax.ppermute(block, 'groups', [(0, 1), (1, 0)])  43.3 us
    ppermute x12, starting transfers between devices, shifted(): lax.ppermute(pieces(k), axis, [(i, (i + k) % num) for i in range(num)])  39.5 us
    all_gather x1, waiting for transfers between devices, local(): whole = lax.all_gather(context, 'head', axis=1, tiled=True)  14.8 us
  transfers between devices with their start and end apart: 19, of which 9 were waited for; matrix products, arithmetic and copies ran while one was open for 8% of the time, Pallas kernels for 54%

profile of v5, /device:TPU:0, one launch (start us, length us, event | category | flops | bytes accessed | tf_op | source)
XLA Modules:
  0.0 546.8 jit_solution(17307107659707174371)
XLA Ops:
  6.5 1.4 fusion.20
  7.9 8.3 %psum.14 = f32[256,1]{0,1:T(1,128)S(1)} all-reduce(f32[256,1]{0,1:T(1,128)S(1)} %bitcast.96), channel_id=1, replica_groups=mesh['groups'=2,'seq'=4,'head'=4] {'head'}, use_global_device_ids=true, to_apply=%region_2.3 | all-reduce | flops 256 | bytes 2048 | tf_op jit(solution)/shard_map/psum | solution.py:24
  18.9 17.5 %collective-permute-start.6 = (bf16[256,1024]{1,0:T(8,128)(2,1)S(1)}, bf16[256,1024]{1,0:T(8,128)(2,1)S(1)}, u32[]{:S(2)}, u32[]{:S(2)}) collective-permute-start(bf16[256,1024]{1,0:T(8,128)(2,1)S(1)} %collective-permute-done.3), channel_id=1, source_target_pairs={{0,3},{1,0},{2,1},{3,2},{4,7},{5,4},{6,5},{7,6},{8,11},{9,8},{10,9... | collective-permute-start | bytes 1572872 | tf_op jit(solution)/shard_map/ppermute | solution.py:17
  36.4 11.7 %collective-permute-start.5 = (bf16[256,1024]{1,0:T(8,128)(2,1)S(1)}, bf16[256,1024]{1,0:T(8,128)(2,1)S(1)}, u32[]{:S(2)}, u32[]{:S(2)}) collective-permute-start(bf16[256,1024]{1,0:T(8,128)(2,1)S(1)} %collective-permute-done.3), channel_id=1, source_target_pairs={{0,2},{1,3},{2,0},{3,1},{4,6},{5,7},{6,4},{7,5},{8,10},{9,11},{10,... | collective-permute-start | bytes 1572872 | tf_op jit(solution)/shard_map/ppermute | solution.py:17
  48.3 23.6 %collective-permute-done.5 = bf16[256,1024]{1,0:T(8,128)(2,1)S(1)} collective-permute-done((bf16[256,1024]{1,0:T(8,128)(2,1)S(1)}, bf16[256,1024]{1,0:T(8,128)(2,1)S(1)}, u32[]{:S(2)}, u32[]{:S(2)}) %collective-permute-start.5) | collective-permute-done | bytes 524320 | tf_op jit(solution)/shard_map/ppermute | solution.py:17
  71.9 3.6 multiply_convert_fusion
  76.2 1.8 collective-permute-start.2
  80.6 2.0 collective-permute-done.1
  84.5 297.9 %shard_map.91 = (bf16[8,1024,128]{2,1,0:T(8,128)(2,1)}, bf16[8,1024,128]{2,1,0:T(8,128)(2,1)}) custom-call(bf16[1024,1024]{1,0:T(8,128)(2,1)} %bitcast.97, bf16[1024,1024]{1,0:T(8,128)(2,1)} %w_key, bf16[1024,1024]{1,0:T(8,128)(2,1)} %w_value), custom_call_target="tpu_custom_call" | custom-call | flops 17179869184 | bytes 524288000 | tf_op jit(solution)/shard_map/pallas_call | solution.py:239
  382.4 4.8 gather_fusion.2
  387.2 3.1 gather_fusion.3
  390.3 7.5 %select_bitcast_fusion.1 = (bf16[8,16,128,128]{3,2,0,1:T(8,128)(2,1)}, bf16[8,16,128,128]{3,2,0,1:T(8,128)(2,1)}) fusion(bf16[16,8,128,128]{3,2,1,0:T(8,128)(2,1)} %gather_fusion.2, pred[16]{0:T(512)(128)(4,1)S(1)} %compare_and_fusion, bf16[16,8,128,128]{3,2,1,0:T(8,128)(2,1)} %gather_fusion.3), kind=kLoop, calls=%fused_computation.9 | loop fusion | flops 4194304 | bytes 16777232 | tf_op jit(solution)/shard_map/jit(_take)/select_n | solution.py:291
  397.8 2.3 gather_fusion.1
  401.0 1.9 copy-done.2
  402.9 3.1 fusion.51
  406.1 2.4 fusion.4
  408.5 2.5 collective-permute-start.9
  411.7 3.0 fusion.16
  414.9 3.2 collective-permute-start.12
  419.4 11.1 %collective-permute-done.12 = bf16[8,4,64,128]{3,2,1,0:T(8,128)(2,1)S(1)} collective-permute-done((bf16[8,4,64,128]{3,2,1,0:T(8,128)(2,1)S(1)}, bf16[8,4,64,128]{3,2,1,0:T(8,128)(2,1)S(1)}, u32[]{:S(2)}, u32[]{:S(2)}) %collective-permute-start.12) | collective-permute-done | bytes 524320 | tf_op jit(solution)/shard_map/ppermute | solution.py:17
  430.5 32.8 %collective-permute-done.11 = bf16[8,4,64,128]{3,2,1,0:T(8,128)(2,1)S(1)} collective-permute-done((bf16[8,4,64,128]{3,2,1,0:T(8,128)(2,1)S(1)}, bf16[8,4,64,128]{3,2,1,0:T(8,128)(2,1)S(1)}, u32[]{:S(2)}, u32[]{:S(2)}) %collective-permute-start.11) | collective-permute-done | bytes 524320 | tf_op jit(solution)/shard_map/ppermute | solution.py:17
  463.3 1.2 fusion.25
  465.9 3.8 constant_dynamic-slice_fusion.1
  470.0 1.7 collective-permute-start.13
  472.0 14.8 %all-gather.3.cloned.1.call-done = bf16[256,4096]{1,0:T(8,128)(2,1)} async-done(((bf16[256,1024]{1,0:T(8,128)(2,1)}), bf16[256,4096]{1,0:T(8,128)(2,1)}) %all-gather.3.cloned.1.call-update) | async-done | bytes 2097168 | tf_op jit(solution)/shard_map/all_gather | solution.py:318
  486.8 1.6 fusion.23
  488.6 3.5 fusion.52
  492.0 3.9 collective-permute-done.15
  496.4 22.1 %collective-permute-done.13 = bf16[1024,512]{1,0:T(8,128)(2,1)} collective-permute-done((bf16[1024,512]{1,0:T(8,128)(2,1)}, bf16[1024,512]{1,0:T(8,128)(2,1)}, u32[]{:S(2)}, u32[]{:S(2)}) %collective-permute-start.13) | collective-permute-done | bytes 1048608 | tf_op jit(solution)/shard_map/ppermute | solution.py:326
  518.6 1.8 convolution_add_fusion.1
  520.4 17.2 %collective-permute-done.14 = bf16[1024,512]{1,0:T(8,128)(2,1)} collective-permute-done((bf16[1024,512]{1,0:T(8,128)(2,1)}, bf16[1024,512]{1,0:T(8,128)(2,1)}, u32[]{:S(2)}, u32[]{:S(2)}) %collective-permute-start.14) | collective-permute-done | bytes 1048608 | tf_op jit(solution)/shard_map/ppermute | solution.py:326
  537.6 1.7 select_convert_fusion.1
  (87 shorter events, 14.3 us)
Async XLA Ops:
  6.5 65.4 %copy-start = (bf16[1024,1024]{1,0:T(8,128)(2,1)S(1)}, bf16[1024,1024]{1,0:T(8,128)(2,1)}, u32[]{:S(2)}) copy-start(bf16[1024,1024]{1,0:T(8,128)(2,1)} %param.13) | copy-start | bytes 6291460
  6.5 391.3 %all-reduce.2.cloned.1.call-start = ((), (), s32[]{:S(2)}) async-start(), calls=%async_computation | async-start | bytes 4194304 | tf_op jit(solution)/shard_map/psum | solution.py:51
  18.2 0.7 collective-permute-start.3
  18.9 29.4 %collective-permute-start.6 = (bf16[256,1024]{1,0:T(8,128)(2,1)S(1)}, bf16[256,1024]{1,0:T(8,128)(2,1)S(1)}, u32[]{:S(2)}, u32[]{:S(2)}) collective-permute-start(bf16[256,1024]{1,0:T(8,128)(2,1)S(1)} %collective-permute-done.3), channel_id=1, source_target_pairs={{0,3},{1,0},{2,1},{3,2},{4,7},{5,4},{6,5},{7,6},{8,11},{9,8},{10,9... | collective-permute-start | bytes 1572872 | tf_op jit(solution)/shard_map/ppermute | solution.py:17
  36.4 35.5 %collective-permute-start.5 = (bf16[256,1024]{1,0:T(8,128)(2,1)S(1)}, bf16[256,1024]{1,0:T(8,128)(2,1)S(1)}, u32[]{:S(2)}, u32[]{:S(2)}) collective-permute-start(bf16[256,1024]{1,0:T(8,128)(2,1)S(1)} %collective-permute-done.3), channel_id=1, source_target_pairs={{0,2},{1,3},{2,0},{3,1},{4,6},{5,7},{6,4},{7,5},{8,10},{9,11},{10,... | collective-permute-start | bytes 1572872 | tf_op jit(solution)/shard_map/ppermute | solution.py:17
  48.1 23.8 %collective-permute-start.4 = (bf16[256,1024]{1,0:T(8,128)(2,1)S(1)}, bf16[256,1024]{1,0:T(8,128)(2,1)S(1)}, u32[]{:S(2)}, u32[]{:S(2)}) collective-permute-start(bf16[256,1024]{1,0:T(8,128)(2,1)S(1)} %collective-permute-done.3), channel_id=1, source_target_pairs={{0,1},{1,2},{2,3},{3,0},{4,5},{5,6},{6,7},{7,4},{8,9},{9,10},{10,1... | collective-permute-start | bytes 1572872 | tf_op jit(solution)/shard_map/ppermute | solution.py:17
  75.5 0.7 copy-start.8
  75.5 0.7 copy-start.9
  75.5 3.3 copy-start.5
  75.6 390.3 %all-gather.5.cloned.1.call-start = ((), (), s32[]{:S(2)}) async-start(), calls=%async_computation.2 | async-start | bytes 5242880 | tf_op jit(solution)/shard_map/all_gather | solution.py:280
  76.2 4.3 collective-permute-start.2
  78.1 4.6 collective-permute-start.1
  78.1 5.6 %collective-permute-start = (s32[4,4]{0,1:T(4,128)S(1)}, s32[4,4]{0,1:T(4,128)S(1)}, u32[]{:S(2)}, u32[]{:S(2)}) collective-permute-start(s32[4,4]{0,1:T(4,128)S(1)} %pad_add_fusion.1), channel_id=1, source_target_pairs={{0,4},{4,8},{8,12},{12,0},{1,5},{5,9},{9,13},{13,1},{2,6},{6,10},{... | collective-permute-start | bytes 200 | tf_op jit(solution)/shard_map/ppermute | solution.py:17
  79.9 406.9 %all-gather.3.cloned.1.call-start = ((), (), s32[]{:S(2)}) async-start(), calls=%async_computation.1 | async-start | bytes 2621440 | tf_op jit(solution)/shard_map/all_gather | solution.py:318
  382.4 4.8 copy-start.3
  400.7 2.2 copy-start.2
  406.1 5.7 %copy-start.4 = (bf16[8,16,128,128]{3,2,0,1:T(8,128)(2,1)S(1)}, bf16[8,16,128,128]{3,2,0,1:T(8,128)(2,1)}, u32[]{:S(2)}) copy-start(bf16[8,16,128,128]{3,2,0,1:T(8,128)(2,1)} %get-tuple-element.33) | copy-start | bytes 12582916
  408.5 10.7 %collective-permute-start.9 = (f32[2,8,4,64]{3,2,1,0:T(4,128)S(1)}, f32[2,8,4,64]{3,2,1,0:T(4,128)S(1)}, u32[]{:S(2)}, u32[]{:S(2)}) collective-permute-start(f32[2,8,4,64]{3,2,1,0:T(4,128)S(1)} %get-tuple-element.27), channel_id=1, source_target_pairs={{0,12},{4,0},{8,4},{12,8},{1,13},{5,1},{9,5},{13,9},{2,14},{6,2},{... | collective-permute-start | bytes 49160 | tf_op jit(solution)/shard_map/ppermute | solution.py:17
  411.1 8.2 %collective-permute-start.8 = (f32[2,8,4,64]{3,2,1,0:T(4,128)S(1)}, f32[2,8,4,64]{3,2,1,0:T(4,128)S(1)}, u32[]{:S(2)}, u32[]{:S(2)}) collective-permute-start(f32[2,8,4,64]{3,2,1,0:T(4,128)S(1)} %get-tuple-element.26), channel_id=1, source_target_pairs={{0,8},{4,12},{8,0},{12,4},{1,9},{5,13},{9,1},{13,5},{2,10},{6,14},... | collective-permute-start | bytes 49160 | tf_op jit(solution)/shard_map/ppermute | solution.py:17
  411.1 8.2 %collective-permute-start.7 = (f32[2,8,4,64]{3,2,1,0:T(4,128)S(1)}, f32[2,8,4,64]{3,2,1,0:T(4,128)S(1)}, u32[]{:S(2)}, u32[]{:S(2)}) collective-permute-start(f32[2,8,4,64]{3,2,1,0:T(4,128)S(1)} %get-tuple-element.25), channel_id=1, source_target_pairs={{0,4},{4,8},{8,12},{12,0},{1,5},{5,9},{9,13},{13,1},{2,6},{6,10},{... | collective-permute-start | bytes 49160 | tf_op jit(solution)/shard_map/ppermute | solution.py:17
  414.9 15.7 %collective-permute-start.12 = (bf16[8,4,64,128]{3,2,1,0:T(8,128)(2,1)S(1)}, bf16[8,4,64,128]{3,2,1,0:T(8,128)(2,1)S(1)}, u32[]{:S(2)}, u32[]{:S(2)}) collective-permute-start(bf16[8,4,64,128]{3,2,1,0:T(8,128)(2,1)S(1)} %get-tuple-element.20), channel_id=1, source_target_pairs={{0,12},{4,0},{8,4},{12,8},{1,13},{5,1},{9,5},{13,9},{2,14},{6,2},{... | collective-permute-start | bytes 1572872 | tf_op jit(solution)/shard_map/ppermute | solution.py:17
  418.1 45.2 %collective-permute-start.11 = (bf16[8,4,64,128]{3,2,1,0:T(8,128)(2,1)S(1)}, bf16[8,4,64,128]{3,2,1,0:T(8,128)(2,1)S(1)}, u32[]{:S(2)}, u32[]{:S(2)}) collective-permute-start(bf16[8,4,64,128]{3,2,1,0:T(8,128)(2,1)S(1)} %get-tuple-element.21), channel_id=1, source_target_pairs={{0,8},{4,12},{8,0},{12,4},{1,9},{5,13},{9,1},{13,5},{2,10},{6,14},... | collective-permute-start | bytes 1572872 | tf_op jit(solution)/shard_map/ppermute | solution.py:17
  419.2 44.1 %collective-permute-start.10 = (bf16[8,4,64,128]{3,2,1,0:T(8,128)(2,1)S(1)}, bf16[8,4,64,128]{3,2,1,0:T(8,128)(2,1)S(1)}, u32[]{:S(2)}, u32[]{:S(2)}) collective-permute-start(bf16[8,4,64,128]{3,2,1,0:T(8,128)(2,1)S(1)} %get-tuple-element.19), channel_id=1, source_target_pairs={{0,4},{4,8},{8,12},{12,0},{1,5},{5,9},{9,13},{13,1},{2,6},{6,10},{... | collective-permute-start | bytes 1572872 | tf_op jit(solution)/shard_map/ppermute | solution.py:17
  465.9 21.0 %copy-start.6 = (bf16[1024,1024]{1,0:T(8,128)(2,1)S(1)}, bf16[1024,1024]{1,0:T(8,128)(2,1)}, u32[]{:S(2)}) copy-start(bf16[1024,1024]{1,0:T(8,128)(2,1)} %param.16) | copy-start | bytes 6291460
  469.7 26.3 %collective-permute-start.15 = (bf16[1024,512]{1,0:T(8,128)(2,1)}, bf16[1024,512]{1,0:T(8,128)(2,1)S(1)}, u32[]{:S(2)}, u32[]{:S(2)}) collective-permute-start(bf16[1024,512]{1,0:T(8,128)(2,1)} %get-tuple-element.17), channel_id=1, source_target_pairs={{0,16},{16,0},{1,17},{17,1},{2,18},{18,2},{3,19},{19,3},{4,20},{20... | collective-permute-start | bytes 3145736 | tf_op jit(solution)/shard_map/ppermute | solution.py:326
  470.0 48.6 %collective-permute-start.13 = (bf16[1024,512]{1,0:T(8,128)(2,1)}, bf16[1024,512]{1,0:T(8,128)(2,1)}, u32[]{:S(2)}, u32[]{:S(2)}) collective-permute-start(bf16[1024,512]{1,0:T(8,128)(2,1)} %get-tuple-element.18), channel_id=1, source_target_pairs={{0,16},{16,0},{1,17},{17,1},{2,18},{18,2},{3,19},{19,3},{4,20},{20... | collective-permute-start | bytes 3145736 | tf_op jit(solution)/shard_map/ppermute | solution.py:326
  471.7 65.9 %collective-permute-start.14 = (bf16[1024,512]{1,0:T(8,128)(2,1)}, bf16[1024,512]{1,0:T(8,128)(2,1)}, u32[]{:S(2)}, u32[]{:S(2)}) collective-permute-start(bf16[1024,512]{1,0:T(8,128)(2,1)} %get-tuple-element.16), channel_id=1, source_target_pairs={{0,16},{16,0},{1,17},{17,1},{2,18},{18,2},{3,19},{19,3},{4,20},{20... | collective-permute-start | bytes 3145736 | tf_op jit(solution)/shard_map/ppermute | solution.py:326
  486.8 1.8 copy-start.7
  518.6 21.7 %copy-start.1 = (bf16[1024,1024]{1,0:T(8,128)(2,1)S(1)}, bf16[1024,1024]{1,0:T(8,128)(2,1)}, u32[]{:S(2)}) copy-start(bf16[1024,1024]{1,0:T(8,128)(2,1)} %param.13) | copy-start | bytes 6291460
Sparse Core Ops, SparseCore 0:
  75.7 130.0 all-reduce.1
  207.4 111.6 all-gather.4
  466.0 20.8 all-gather.2
